TPU v7x, 512 devices: a whole 4x4x16 slice. The times are simulated.
512 devices in a mesh: dp: 32 (over x, y, core), ctx: 16 (over z).
Axes of the slice: x: 4, y: 4, z: 16, core: 2. Of those that a mesh axis runs over, the one named last changes fastest.
Arguments:
- prompt_kv: bfloat16 [32, 2048, 256], P('dp', 'ctx'), may hold values from -6 to 6
- queries: bfloat16 [32, 2048, 1024], P('dp', 'ctx'), may hold values from -9 to 9
- branch_kv: bfloat16 [32, 2048, 256], P('dp', 'ctx'), may hold values from -6 to 6
- dout: bfloat16 [32, 2048, 1024], P('dp', 'ctx'), may hold values from -6 to 6
- prefix: int32 [32, 32], P('dp'), may hold values from 1 to 16
Outputs:
- query_grad: bfloat16 [32, 2048, 1024], P('dp', 'ctx')
- prompt_kv_grad: bfloat16 [32, 2048, 256], P('dp', 'ctx')
- branch_kv_grad: bfloat16 [32, 2048, 256], P('dp', 'ctx')
- bias_grad: float32 [1280], replicated
Inputs may be any that keep to these rules, and one draw needn't show every extreme that they name: Branch b of group g consists of rows b * 64 to b * 64 + 63 and sees prompt positions below prefix * 128.
All inputs are finite; a program needn't handle non-finite values.
Results may differ from a plain program's by a relative error of at most 0.0063.
Values may be sent and summed in bfloat16 or wider, within the bound.
No kernel may reach another device: no remote copies, remote signals or barrier semaphores. Data moves between devices by JAX's collectives and lax.ppermute only.
A program may use at most 64 MiB of HBM per device.

v0:
```python
import jax
import jax.numpy as jnp
from jax import lax
from jax.sharding import PartitionSpec as P

BLK = 64
KBLK = 128


NEG_FILL = -1e30


def masked_scores(heads_q, heads_do, key_slab, positions, limits, score_scale):
    head_width = heads_q.shape[2]
    key_rows = key_slab[:, :head_width]
    value_rows = key_slab[:, head_width:]
    scores = (
        jnp.einsum("rhd,jd->rhj", heads_q, key_rows, preferred_element_type=jnp.float32)
        * score_scale
    )
    visible = (positions[None, :] < limits[:, None])[:, None, :]
    scores = jnp.where(visible, scores, NEG_FILL)
    grad_dots = jnp.einsum("rhd,jd->rhj", heads_do, value_rows, preferred_element_type=jnp.float32)
    return (scores, grad_dots, visible)


def absorb(softmax_stats, heads_q, heads_do, key_slab, positions, limits, score_scale):
    running_max, total_mass, dot_mass = softmax_stats
    scores, grad_dots, visible = masked_scores(
        heads_q, heads_do, key_slab, positions, limits, score_scale
    )
    new_max = jnp.maximum(running_max, scores.max(-1))
    weights = jnp.where(visible, jnp.exp(scores - new_max[..., None]), 0.0)
    factor = jnp.exp(running_max - new_max)
    return (
        new_max,
        total_mass * factor + weights.sum(-1),
        dot_mass * factor + (weights * grad_dots).sum(-1),
    )


def slab_probs(heads_q, heads_do, key_slab, positions, limits, log_total, row_delta, score_scale):
    scores, grad_dots, visible = masked_scores(
        heads_q, heads_do, key_slab, positions, limits, score_scale
    )
    prob_full = jnp.where(visible, jnp.exp(scores - log_total[..., None]), 0.0)
    dscores = prob_full * (grad_dots - row_delta[..., None])
    return (prob_full.astype(jnp.bfloat16), dscores.astype(jnp.bfloat16))


def query_term(dscores, key_slab, head_width):
    return jnp.einsum(
        "rhj,jd->rhd", dscores, key_slab[:, :head_width], preferred_element_type=jnp.float32
    )


def key_term(prob_bf, dscores, heads_q, heads_do, score_scale):
    key_grad = (
        jnp.einsum("rhj,rhd->jd", dscores, heads_q, preferred_element_type=jnp.float32)
        * score_scale
    )
    value_grad = jnp.einsum("rhj,rhd->jd", prob_bf, heads_do, preferred_element_type=jnp.float32)
    return jnp.concatenate([key_grad, value_grad], 1)


def body(prompt_kv, queries, branch_kv, dout, prefix):
    shard_keys = prompt_kv.shape[1]
    row_count = queries.shape[1]
    head_width = branch_kv.shape[2] // 2
    head_count = queries.shape[2] // head_width
    score_scale = head_width ** (-0.5)
    ctx_ranks = lax.axis_size("ctx")
    ctx_place = lax.axis_index("ctx")
    total_keys = shard_keys * ctx_ranks
    slab_keys = 512
    slab_count = total_keys // slab_keys
    block_count = row_count // BLK
    heads_q = queries[0].reshape(row_count, head_count, head_width)
    heads_do = dout[0].reshape(row_count, head_count, head_width)
    all_limits = jnp.repeat(prefix[0], BLK) * KBLK
    limits = lax.dynamic_slice_in_dim(all_limits, ctx_place * row_count, row_count)
    within = jnp.arange(BLK, dtype=jnp.int32)
    causal = (within[None, :] <= within[:, None])[None, :, None, :]
    group_q = heads_q.reshape(block_count, BLK, head_count, head_width)
    group_do = heads_do.reshape(block_count, BLK, head_count, head_width)
    own_keys = branch_kv[0, :, :head_width].reshape(block_count, BLK, head_width)
    own_values = branch_kv[0, :, head_width:].reshape(block_count, BLK, head_width)
    own_scores = (
        jnp.einsum("bihd,bjd->bihj", group_q, own_keys, preferred_element_type=jnp.float32)
        * score_scale
    )
    own_scores = jnp.where(causal, own_scores, NEG_FILL)
    own_dots = jnp.einsum(
        "bihd,bjd->bihj", group_do, own_values, preferred_element_type=jnp.float32
    )
    own_max = own_scores.max(-1)
    own_weights = jnp.where(causal, jnp.exp(own_scores - own_max[..., None]), 0.0)
    softmax_stats = (
        own_max.reshape(row_count, head_count),
        own_weights.sum(-1).reshape(row_count, head_count),
        (own_weights * own_dots).sum(-1).reshape(row_count, head_count),
    )
    gathered = lax.all_gather(prompt_kv, "ctx", axis=1, tiled=True)[0]
    slabs = gathered.reshape(slab_count, slab_keys, 2 * head_width)
    slab_starts = jnp.arange(slab_count, dtype=jnp.int32) * slab_keys

    def stats_step(running, inputs):
        key_slab, first_key = inputs
        positions = first_key + jnp.arange(slab_keys, dtype=jnp.int32)
        return (absorb(running, heads_q, heads_do, key_slab, positions, limits, score_scale), None)

    softmax_stats, unused = lax.scan(stats_step, softmax_stats, (slabs, slab_starts))
    running_max, total_mass, dot_mass = softmax_stats
    log_total = running_max + jnp.log(total_mass)
    row_delta = dot_mass / total_mass
    grouped_log = log_total.reshape(block_count, BLK, head_count)[..., None]
    grouped_delta = row_delta.reshape(block_count, BLK, head_count)[..., None]
    own_probs = jnp.where(causal, jnp.exp(own_scores - grouped_log), 0.0)
    own_ds = (own_probs * (own_dots - grouped_delta)).astype(jnp.bfloat16)
    own_probs = own_probs.astype(jnp.bfloat16)
    own_query = jnp.einsum("bihj,bjd->bihd", own_ds, own_keys, preferred_element_type=jnp.float32)
    own_query = own_query.reshape(row_count, head_count, head_width)
    own_key_grad = (
        jnp.einsum("bihj,bihd->bjd", own_ds, group_q, preferred_element_type=jnp.float32)
        * score_scale
    )
    own_value_grad = jnp.einsum(
        "bihj,bihd->bjd", own_probs, group_do, preferred_element_type=jnp.float32
    )
    branch_grad = jnp.concatenate([own_key_grad, own_value_grad], 2).reshape(
        row_count, 2 * head_width
    )
    query_start = jnp.zeros((row_count, head_count, head_width), jnp.float32)

    def both_step(running, inputs):
        key_slab, first_key = inputs
        positions = first_key + jnp.arange(slab_keys, dtype=jnp.int32)
        prob_bf, dscores = slab_probs(
            heads_q, heads_do, key_slab, positions, limits, log_total, row_delta, score_scale
        )
        return (
            running + query_term(dscores, key_slab, head_width),
            key_term(prob_bf, dscores, heads_q, heads_do, score_scale),
        )

    prompt_query, grad_terms = lax.scan(both_step, query_start, (slabs, slab_starts))
    grad_terms = grad_terms.reshape(1, total_keys, 2 * head_width)
    kv_grad = lax.psum_scatter(grad_terms, "ctx", scatter_dimension=1, tiled=True)[0]
    query_grad = (prompt_query + own_query) * score_scale
    bias_term = jnp.concatenate(
        [query_grad.sum(0).reshape(-1), kv_grad.sum(0) + branch_grad.sum(0)]
    )
    bias_grad = lax.psum(bias_term, ("dp", "ctx"))
    return (
        query_grad.reshape(1, row_count, head_count * head_width).astype(jnp.bfloat16),
        kv_grad[None].astype(jnp.bfloat16),
        branch_grad[None].astype(jnp.bfloat16),
        bias_grad,
    )


def solution(mesh):
    placed = (
        P("dp", "ctx", None),
        P("dp", "ctx", None),
        P("dp", "ctx", None),
        P("dp", "ctx", None),
        P("dp", None),
    )
    return jax.shard_map(
        body,
        mesh=mesh,
        in_specs=placed,
        out_specs=(P("dp", "ctx", None), P("dp", "ctx", None), P("dp", "ctx", None), P()),
        check_vma=False,
    )
```

profile of v0, /device:TPU:1, one launch (start us, length us, event | category | flops | bytes accessed | tf_op | source)
XLA Modules:
  0.0 308.0 jit_solution(2355395227697126825)
XLA Ops:
  8.8 1.1 copy.35
  9.9 1.0 copy.73
  10.9 1.2 copy.33
  12.2 1.0 copy.72
  14.8 62.2 %all-gather.2.cloned.1.call-done = bf16[1,2048,256]{2,1,0:T(8,128)(2,1)} async-done(((bf16[1,128,256]{2,1,0:T(8,128)(2,1)}), bf16[1,2048,256]{2,1,0:T(8,128)(2,1)}) %all-gather.2.cloned.1.call-update) | async-done | bytes 1048592 | tf_op jit(solution)/shard_map/all_gather | solution.py:103
  77.0 16.6 %while.27 = (s32[]{:T(128)}, f32[128,8]{0,1:T(8,128)S(1)}, f32[128,8]{0,1:T(8,128)S(1)}, f32[128,8]{0,1:T(8,128)S(1)}, s32[4]{0:T(128)S(1)}, /*index=5*/s32[128]...) while((s32[]{:T(128)}, f32[128,8]{0,1:T(8,128)S(1)}, ...), condition=%wide.region_7.8_spmd, body=%wide.region_3.7_spmd.sunk | while | flops 275844608 | bytes 7942785 | solution.py:112
  78.4 1.0 dynamic-slice_bitcast_fusion.4
  79.8 0.7 fusion.65
  82.5 1.0 dynamic-slice_bitcast_fusion.4
  86.7 1.0 dynamic-slice_bitcast_fusion.4
  90.8 1.0 dynamic-slice_bitcast_fusion.4
  93.6 24.7 %while.28 = (s32[]{:T(128)}, f32[128,8,128]{2,0,1:T(8,128)S(1)}, f32[4,512,256]{2,1,0:T(8,128)}, s32[4]{0:T(128)S(1)}, s32[128]{0:T(128)S(1)}, /*index=5*/bf16[4...) while((s32[]{:T(128)}, f32[128,8,128]{2,0,1:T(8,128)S(1)}, ...), condition=%wide.region_9.10_spmd.clone, body=%wide.region_8.9_spmd.clone.sunk | while | flops 675807744 | bytes 16265887 | solution.py:146
  95.0 1.0 dynamic-slice_bitcast_fusion.5
  98.9 0.8 constant_dynamic-update-slice_fusion.2
  101.1 1.0 dynamic-slice_bitcast_fusion.5
  105.1 0.8 constant_dynamic-update-slice_fusion.2
  107.3 1.0 dynamic-slice_bitcast_fusion.5
  111.3 0.9 constant_dynamic-update-slice_fusion.2
  113.5 1.0 dynamic-slice_bitcast_fusion.5
  117.5 0.9 constant_dynamic-update-slice_fusion.2
  119.5 0.8 convert_element_type.45
  121.7 66.1 %reduce-scatter.2.cloned.1.call-done = f32[1,128,256]{2,1,0:T(8,128)} async-done(((f32[1,2048,256]{2,1,0:T(8,128)}), f32[1,128,256]{2,1,0:T(8,128)}) %reduce-scatter.2.cloned.1.call-update) | async-done | bytes 131088 | tf_op jit(solution)/shard_map/reduce_scatter | solution.py:148
  187.8 1.6 fusion.29
  189.4 111.7 %psum.7 = f32[1280]{0:T(1024)} all-reduce(f32[1280]{0:T(1024)S(1)} %pad_maximum_fusion.1), channel_id=1, replica_groups=mesh['dp'=32,'ctx'=16] {'dp','ctx'}, use_global_device_ids=true, to_apply=%region_14.15 | all-reduce | flops 1280 | bytes 10240 | tf_op jit(solution)/shard_map/psum | solution.py:153
  (118 shorter events, 34.4 us)
Async XLA Ops:
  7.2 6.4 %copy-start.4 = (bf16[1,128,256]{2,1,0:T(8,128)(2,1)S(1)}, bf16[1,128,256]{2,1,0:T(8,128)(2,1)}, u32[]{:S(2)}) copy-start(bf16[1,128,256]{2,1,0:T(8,128)(2,1)} %param.11) | copy-start | bytes 196612
  7.2 69.8 %all-gather.2.cloned.1.call-start = ((), (), s32[]{:S(2)}) async-start(), calls=%async_computation.1 | async-start | bytes 1114112 | tf_op jit(solution)/shard_map/all_gather | solution.py:103
  7.9 179.9 %reduce-scatter.2.cloned.1.call-start = ((), (), s32[]{:S(2)}) async-start(), calls=%async_computation.2 | async-start | bytes 2228224 | tf_op jit(solution)/shard_map/reduce_scatter | solution.py:148
  10.9 3.7 %copy-start.2 = (bf16[16,8,8,128]{3,2,1,0:T(8,128)(2,1)}, bf16[16,8,8,128]{3,2,1,0:T(8,128)(2,1)S(1)}, u32[]{:S(2)}) copy-start(bf16[16,8,8,128]{3,2,1,0:T(8,128)(2,1)S(1)} %copy.73) | copy-start | bytes 786436
  13.2 63.8 %copy-start = (bf16[16,8,8,128]{3,2,1,0:T(8,128)(2,1)}, bf16[16,8,8,128]{3,2,1,0:T(8,128)(2,1)S(1)}, u32[]{:S(2)}) copy-start(bf16[16,8,8,128]{3,2,1,0:T(8,128)(2,1)S(1)} %copy.72) | copy-start | bytes 786436
  118.5 1.7 copy-start.3
  119.1 1.6 copy-start.1
Sparse Core Ops, SparseCore 0:
  10.1 66.8 all-gather.1
  118.5 69.3 reduce-scatter.1
where the time goes:
time: 309 us; the launch traced here: 308 us
  waiting for transfers between devices  129 us (42%)
  blocking collectives  112 us (36%)
  local copies, waits for them, and re-layouts  23 us (7%)
  matrix products  17.4 us (6%)
  between operations  14.2 us (5%)
  other arithmetic  12 us (4%)
    psum x1, blocking collectives, body(): bias_grad = lax.psum(bias_term, ('dp', 'ctx'))  112 us
    reduce_scatter x1, waiting for transfers between devices, body(): lax.psum_scatter(grad_terms, 'ctx', scatter_dimension=1, tiled=True)[0]  66.1 us
    all_gather x1, waiting for transfers between devices, body(): gathered = lax.all_gather(prompt_kv, 'ctx', axis=1, tiled=True)[0]  62.2 us
    squeeze x8, local copies, waits for them, and re-layouts, body(): lax.scan(stats_step, softmax_stats, (slabs, slab_starts))  7.79 us
  transfers between devices with their start and end apart: 2, of which 2 were waited for; matrix products, arithmetic and copies ran while one was open for 3% of the time, Pallas kernels for 0%

commit v1 on v0

v1 whole, which is shorter than its diff:
```python
import functools
import math

import jax
import jax.numpy as jnp
from jax import lax
from jax.experimental import pallas as pl
from jax.experimental.pallas import tpu as pltpu
from jax.sharding import Mesh
from jax.sharding import PartitionSpec as P

BLK = 64
KBLK = 128
BP = 256
NEG = -1e30
DP = ("x", "y", "c")
CTX = ("zh", "zl")
F32 = jnp.float32
BF16 = jnp.bfloat16


def mm(a, b):
    return jnp.dot(a, b, preferred_element_type=F32)


def turn(a):
    return a.astype(F32).T.astype(BF16)


def grads_kernel(
    info, q_ref, do_ref, bkv_ref, kv_ref,
    dq_ref, bg_ref, send_ref, keep_ref, bias_ref,
    qs, dos, qt, dot_, e_s, d_s, m_s, l_s, w_s, f_s, acc,
):
    heads = q_ref.shape[1] // 128
    nb = q_ref.shape[0] // BLK
    wide = heads * BLK
    rows = nb * wide
    total = kv_ref.shape[1]
    nblk = total // BP
    scale = 128 ** -0.5
    c = scale * math.log2(math.e)
    for b in range(nb):
        for h in range(heads):
            at = (b * heads + h) * BLK
            qs[at:at + BLK, :] = q_ref[b * BLK:(b + 1) * BLK, h * 128:(h + 1) * 128]
            dos[at:at + BLK, :] = do_ref[b * BLK:(b + 1) * BLK, h * 128:(h + 1) * 128]
    qt[...] = turn(qs[...])
    dot_[...] = turn(dos[...])

    def first(blk, carry):
        at = pl.multiple_of(blk * BP, BP)
        k = kv_ref[0, pl.ds(at, BP), :]
        v = kv_ref[1, pl.ds(at, BP), :]
        pos = blk * BP + lax.broadcasted_iota(jnp.int32, (BP, wide), 0)
        for b in range(nb):
            cols = slice(b * wide, (b + 1) * wide)
            s = mm(k, qt[:, cols]) * c
            s = jnp.where(pos < info[b] * KBLK, s, NEG)
            m = s.max(0, keepdims=True)
            e = jnp.exp2(s - m)
            d = mm(v, dot_[:, cols])
            e_s[pl.ds(at, BP), cols] = e
            d_s[pl.ds(at, BP), cols] = d
            m_s[pl.ds(blk, 1), cols] = m
            l_s[pl.ds(blk, 1), cols] = e.sum(0, keepdims=True)
            w_s[pl.ds(blk, 1), cols] = (e * d).sum(0, keepdims=True)
        return carry

    lax.fori_loop(0, nblk, first, 0)

    own = []
    row_in = lax.broadcasted_iota(jnp.int32, (BLK, wide), 1) % BLK
    key_in = lax.broadcasted_iota(jnp.int32, (BLK, wide), 0)
    causal = key_in <= row_in
    for b in range(nb):
        cols = slice(b * wide, (b + 1) * wide)
        bk = bkv_ref[b * BLK:(b + 1) * BLK, :128]
        bv = bkv_ref[b * BLK:(b + 1) * BLK, 128:]
        s = jnp.where(causal, mm(bk, qt[:, cols]) * c, NEG)
        m = s.max(0, keepdims=True)
        e = jnp.exp2(s - m)
        d = mm(bv, dot_[:, cols])
        top = jnp.maximum(m, m_s[:, cols].max(0, keepdims=True))
        scales = jnp.exp2(m_s[:, cols] - top)
        mine = jnp.exp2(m - top)
        mass = (l_s[:, cols] * scales).sum(0, keepdims=True) + e.sum(0, keepdims=True) * mine
        dots = (w_s[:, cols] * scales).sum(0, keepdims=True) + (e * d).sum(0, keepdims=True) * mine
        inv = 1.0 / mass
        delta = dots * inv
        f_s[:nblk, cols] = scales * inv
        f_s[nblk:nblk + 1, cols] = delta
        p = e * (mine * inv)
        ds = (p * (d - delta)).astype(BF16)
        p = p.astype(BF16)
        own_k = mm(ds, qs[cols, :]) * scale
        own_v = mm(p, dos[cols, :])
        bg_ref[b * BLK:(b + 1) * BLK, :128] = own_k.astype(BF16)
        bg_ref[b * BLK:(b + 1) * BLK, 128:] = own_v.astype(BF16)
        own.append((own_k.sum(0, keepdims=True), own_v.sum(0, keepdims=True)))
        acc[:, cols] = mm(turn(bk), ds)

    delta = f_s[nblk:nblk + 1, :]
    even = info[nb] == 0

    def second(blk, carry):
        sum_k, sum_v = carry
        at = pl.multiple_of(blk * BP, BP)
        p = e_s[pl.ds(at, BP), :] * f_s[pl.ds(blk, 1), :]
        ds = (p * (d_s[pl.ds(at, BP), :] - delta)).astype(BF16)
        p = p.astype(BF16)
        dk = mm(ds, qs[...]) * scale
        dv = mm(p, dos[...])
        acc[...] += mm(turn(kv_ref[0, pl.ds(at, BP), :]), ds)
        keep_ref[pl.ds(at, BP), :] = jnp.where(even, dk, dv)
        send_ref[pl.ds(at, BP), :] = jnp.where(even, dv, dk).astype(BF16)
        return (sum_k + dk.sum(0, keepdims=True), sum_v + dv.sum(0, keepdims=True))

    start = (sum(o[0] for o in own), sum(o[1] for o in own))
    sum_k, sum_v = lax.fori_loop(0, nblk, second, start)
    bias_ref[...] = jnp.zeros_like(bias_ref)
    bias_ref[heads:heads + 1, :] = sum_k
    bias_ref[heads + 1:heads + 2, :] = sum_v
    dq = acc[...].T * scale
    for h in range(heads):
        part = jnp.zeros((1, 128), F32)
        for b in range(nb):
            at = (b * heads + h) * BLK
            piece = dq[at:at + BLK, :]
            part += piece.sum(0, keepdims=True)
            dq_ref[b * BLK:(b + 1) * BLK, h * 128:(h + 1) * 128] = piece.astype(BF16)
        bias_ref[h:h + 1, :] = part


def grads(info, q, do, bkv, kv):
    rows, width = q.shape
    total = kv.shape[1]
    wide = rows * width // 128
    nblk = total // BP
    vmem = pl.BlockSpec(memory_space=pltpu.VMEM)
    return pl.pallas_call(
        grads_kernel,
        out_shape=(
            jax.ShapeDtypeStruct((rows, width), BF16),
            jax.ShapeDtypeStruct((rows, 256), BF16),
            jax.ShapeDtypeStruct((total, 128), BF16),
            jax.ShapeDtypeStruct((total, 128), F32),
            jax.ShapeDtypeStruct((16, 128), F32),
        ),
        in_specs=[pl.BlockSpec(memory_space=pltpu.SMEM)] + [vmem] * 4,
        out_specs=(vmem,) * 5,
        scratch_shapes=[
            pltpu.VMEM((wide, 128), BF16),
            pltpu.VMEM((wide, 128), BF16),
            pltpu.VMEM((128, wide), BF16),
            pltpu.VMEM((128, wide), BF16),
            pltpu.VMEM((total, wide), F32),
            pltpu.VMEM((total, wide), F32),
            pltpu.VMEM((nblk, wide), F32),
            pltpu.VMEM((nblk, wide), F32),
            pltpu.VMEM((nblk, wide), F32),
            pltpu.VMEM((nblk + 8, wide), F32),
            pltpu.VMEM((128, wide), F32),
        ],
        compiler_params=pltpu.CompilerParams(vmem_limit_bytes=40 * 2**20),
        cost_estimate=pl.CostEstimate(
            flops=10 * wide * total * 128, bytes_accessed=3 * 2**20, transcendentals=wide * total
        ),
    )(info, q, do, bkv, kv)


def body(prompt_kv, queries, branch_kv, dout, prefix):
    n = lax.axis_size(CTX)
    place = lax.axis_index(CTX)
    rows = queries.shape[1]
    nb = rows // BLK
    keys = prompt_kv.shape[1]
    halves = prompt_kv[0].reshape(keys, 2, 128).transpose(1, 0, 2)
    out = jnp.broadcast_to(halves[None], (n // 2, 2, keys, 128)).reshape(n, keys, 128)
    mine = lax.all_to_all(out, CTX, 0, 0, tiled=True).reshape(1, n * keys, 128)
    kv = lax.all_gather(mine, "zl", axis=0, tiled=True)
    mine_prefix = lax.dynamic_slice_in_dim(prefix[0], place * nb, nb)
    info = jnp.concatenate([mine_prefix, lax.axis_index("zl").reshape(1)])
    dq, bg, send, keep, bias = grads(info, queries[0], dout[0], branch_kv[0], kv)
    got = lax.ppermute(send, "zl", [(0, 1), (1, 0)])
    bias = lax.psum(bias, "c")
    flat = lax.axis_size(("x", "y"))
    bias = lax.all_to_all(
        jnp.broadcast_to(bias[None], (flat, 16, 128)), ("x", "y"), 0, 0, tiled=True
    ).sum(0)
    high = bias.astype(BF16)
    low = (bias - high.astype(F32)).astype(BF16)
    extra = jnp.concatenate([high, low], 0)
    pair = (keep + got.astype(F32)).astype(BF16).reshape(n, keys, 128)
    parcel = jnp.concatenate([pair, jnp.broadcast_to(extra[None], (n, 32, 128))], 1)
    parcel = lax.all_to_all(parcel, CTX, 0, 0, tiled=True).astype(F32)
    sums = parcel.reshape(n // 2, 2, keys + 32, 128).sum(0)
    kv_grad = jnp.concatenate([sums[0, :keys], sums[1, :keys]], 1)
    bias = sums[:, keys:].sum(0)
    bias = (bias[:10] + bias[16:26]).reshape(-1)
    return dq[None], kv_grad[None].astype(BF16), bg[None], bias


def solution(mesh):
    fine = Mesh(
        mesh.devices.reshape(4, 4, 2, mesh.shape["ctx"] // 2, 2), ("x", "y", "c", "zh", "zl")
    )
    split = P(DP, CTX, None)
    return jax.shard_map(
        body,
        mesh=fine,
        in_specs=(split, split, split, split, P(DP, None)),
        out_specs=(split, split, split, P()),
        check_vma=False,
    )
```

time: 309 us -> 167 us (0.54)
  waiting for transfers between devices: 129 us -> 33.7 us
  local copies, waits for them, and re-layouts: 23 us -> 2.33 us
  matrix products: 17.4 us -> 0 us
  blocking collectives: 112 us -> 100 us
  Pallas kernels: 0 us -> 10.6 us
  other arithmetic: 12 us -> 1.61 us
    psum x1, blocking collectives: 112 us -> 3.04 us  [body(): bias = lax.psum(bias, 'c')]
    all_to_all x0 -> x3, blocking collectives: none -> 97.4 us  [the longest x1 45.5 us: body(): parcel = lax.all_to_all(parcel, CTX, 0, 0, tiled=True).astype(F32)]
    reduce_scatter x1 -> x0, waiting for transfers between devices: 66.1 us -> none  [body(): lax.psum_scatter(grad_terms, 'ctx', scatter_dimension=1, tiled=True)[0]]
    all_gather x1, waiting for transfers between devices: 62.2 us -> 33.7 us  [body(): kv = lax.all_gather(mine, 'zl', axis=0, tiled=True)]
    dot_general x33 -> x0, matrix products: 17.4 us -> none  [the longest x8 4.68 us: masked_scores(): jnp.einsum('rhd,jd->rhj', heads_do, value_rows, preferred_element_type=jn...]
    pallas_call x0 -> x1, Pallas kernels: none -> 10.6 us  [grads(): pl.pallas_call(grads_kernel, out_shape=(jax.ShapeDtypeStruct((rows, width...]
    squeeze x8 -> x0, local copies, waits for them, and re-layouts: 7.79 us -> none  [body(): lax.scan(stats_step, softmax_stats, (slabs, slab_starts))]
    add x13 -> x0, other arithmetic: 5.22 us -> none  [the longest x4 2.59 us: both_step(): positions = first_key + jnp.arange(slab_keys, dtype=jnp.int32)]
  transfers between devices with their start and end apart: 2 -> 2, of which waited for: 2 -> 1; matrix products, arithmetic and copies ran while one was open for 3% -> 0% of each run, Pallas kernels for 0% -> 0%
where the time goes in v1:
time: 167 us; the launch traced here: 165 us
  blocking collectives  100 us (60%)
  waiting for transfers between devices  33.7 us (20%)
  between operations  14.2 us (9%)
  Pallas kernels  10.6 us (6%)
  local copies, waits for them, and re-layouts  2.33 us (1%)
  starting transfers between devices  1.95 us (1%)
    all_to_all x1, blocking collectives, body(): parcel = lax.all_to_all(parcel, CTX, 0, 0, tiled=True).astype(F32)  45.5 us
    all_to_all x1, blocking collectives, body(): mine = lax.all_to_all(out, CTX, 0, 0, tiled=True).reshape(1, n * keys, 128)  38.6 us
    all_gather x1, waiting for transfers between devices, body(): kv = lax.all_gather(mine, 'zl', axis=0, tiled=True)  33.7 us
    all_to_all x1, blocking collectives, body(): lax.all_to_all(jnp.broadcast_to(bias[None], (flat, 16, 128)), ('x', 'y'),...  13.3 us
    pallas_call x1, Pallas kernels, grads(): pl.pallas_call(grads_kernel, out_shape=(jax.ShapeDtypeStruct((rows, width...  10.6 us
  transfers between devices with their start and end apart: 2, of which 1 were waited for; matrix products, arithmetic and copies ran while one was open for 0% of the time, Pallas kernels for 0%

profile of v1, /device:TPU:1, one launch (start us, length us, event | category | flops | bytes accessed | tf_op | source)
XLA Modules:
  0.0 164.8 jit_solution(609013935627040140)
XLA Ops:
  7.2 0.0 copy-start
  7.2 0.0 all-gather.2.cloned.1.call-start
  7.2 0.9 reshape_squeeze.3
  8.1 0.0 copy-start.2
  8.1 0.0 copy-start.3
  8.1 0.0 copy-start.4
  8.1 0.1 broadcast_in_dim.10
  8.2 38.6 %all_to_all.15 = bf16[16,128,128]{2,1,0:T(8,128)(2,1)} all-to-all(bf16[16,128,128]{2,1,0:T(8,128)(2,1)S(1)} %bitcast.21), channel_id=1, replica_groups=mesh['x'=4,'y'=4,'c'=2,'zh'=8,'zl'=2] {'zh','zl'}, dimensions={0} | all-to-all | bytes 1048576 | tf_op jit(solution)/shard_map/all_to_all | solution.py:180
  46.9 0.0 all-gather.2.cloned.1.call-update
  46.9 0.1 dynamic-slice_bitcast_fusion
  47.0 0.1 pad_add_fusion.info
  47.0 33.7 %all-gather.2.cloned.1.call-done.kv_ref = bf16[2,2048,128]{2,1,0:T(8,128)(2,1)} async-done(((bf16[1,2048,128]{2,1,0:T(8,128)(2,1)}), bf16[2,2048,128]{2,1,0:T(8,128)(2,1)}) %all-gather.2.cloned.1.call-update) | async-done | bytes 1048592 | tf_op jit(solution)/shard_map/all_gather | solution.py:181
  80.7 0.0 copy-done.4
  80.8 1.2 copy-done.1
  82.0 10.6 %shard_map.84 = (bf16[128,1024]{1,0:T(8,128)(2,1)}, bf16[128,256]{1,0:T(8,128)(2,1)}, bf16[2048,128]{1,0:T(8,128)(2,1)S(1)}, f32[2048,128]{1,0:T(8,128)S(1)}, f32[16,128]{1,0:T(8,128)S(1)}) custom-call(s32[3]{0:T(128)S(1)} %pad_add_fusion.info, bf16[128,1024]{1,0:T(8,128)(2,1)S(1)} %bitcast.16, bf16[128,1024]{1,0:T(8,128)(2,1)S(1)} %bitcast.17, ...), custom_call_target="tpu_custom_call" | custom-call | flops 2684354560 | bytes 3145728 | tf_op jit(solution)/shard_map/pallas_call | solution.py:141
  92.6 1.9 %collective-permute-start = (bf16[2048,128]{1,0:T(8,128)(2,1)S(1)}, bf16[2048,128]{1,0:T(8,128)(2,1)S(1)}, u32[]{:S(2)}, u32[]{:S(2)}) collective-permute-start(bf16[2048,128]{1,0:T(8,128)(2,1)S(1)} %get-tuple-element.11), channel_id=1, source_target_pairs={{0,1},{1,0},{2,3},{3,2},{4,5},{5,4},{6,7},{7,6},{8,9},{9,8},{10,11... | collective-permute-start | bytes 1572872 | tf_op jit(solution)/shard_map/ppermute | solution.py:185
  94.5 3.0 %psum.7 = f32[16,128]{1,0:T(8,128)S(1)} all-reduce(f32[16,128]{1,0:T(8,128)S(1)} %get-tuple-element.12), channel_id=1, replica_groups=mesh['x'=4,'y'=4,'c'=2,'zh'=8,'zl'=2] {'c'}, use_global_device_ids=true, to_apply=%region_0.0 | all-reduce | flops 2048 | bytes 16384 | tf_op jit(solution)/shard_map/psum | solution.py:186
  97.6 13.3 %all_to_all.16 = f32[16,16,128]{2,1,0:T(8,128)S(1)} all-to-all(f32[16,16,128]{2,1,0:T(8,128)S(1)} %broadcast_in_dim.12), channel_id=1, replica_groups=mesh['x'=4,'y'=4,'c'=2,'zh'=8,'zl'=2] {'x','y'}, dimensions={0} | all-to-all | bytes 262144 | tf_op jit(solution)/shard_map/all_to_all | solution.py:188
  110.9 0.0 collective-permute-done
  110.9 0.1 add_convert_fusion
  111.1 45.5 %all_to_all.17 = bf16[16,160,128]{2,1,0:T(8,128)(2,1)S(1)} all-to-all(bf16[16,160,128]{2,1,0:T(8,128)(2,1)S(1)} %pad_maximum_fusion), channel_id=1, replica_groups=mesh['x'=4,'y'=4,'c'=2,'zh'=8,'zl'=2] {'zh','zl'}, dimensions={0} | all-to-all | bytes 1310720 | tf_op jit(solution)/shard_map/all_to_all | solution.py:196
  156.6 0.1 convert_reduce_fusion
  156.7 0.6 fusion
  157.3 0.6 pad_maximum_fusion.1
  (14 shorter events, 0.2 us)
Async XLA Ops:
  7.2 39.7 %copy-start = (s32[1,32]{1,0:T(1,128)S(1)}, s32[1,32]{1,0:T(1,128)}, u32[]{:S(2)}) copy-start(s32[1,32]{1,0:T(1,128)} %param.9) | copy-start | bytes 388
  7.2 73.6 %all-gather.2.cloned.1.call-start = ((), (), s32[]{:S(2)}) async-start(), calls=%async_computation.3 | async-start | bytes 1572864 | tf_op jit(solution)/shard_map/all_gather | solution.py:181
  8.1 72.6 %copy-start.2 = (bf16[1,128,1024]{2,1,0:T(8,128)(2,1)S(1)}, bf16[1,128,1024]{2,1,0:T(8,128)(2,1)}, u32[]{:S(2)}) copy-start(bf16[1,128,1024]{2,1,0:T(8,128)(2,1)} %param.6) | copy-start | bytes 786436
  8.1 72.6 %copy-start.3 = (bf16[1,128,1024]{2,1,0:T(8,128)(2,1)S(1)}, bf16[1,128,1024]{2,1,0:T(8,128)(2,1)}, u32[]{:S(2)}) copy-start(bf16[1,128,1024]{2,1,0:T(8,128)(2,1)} %param.8) | copy-start | bytes 786436
  8.1 72.6 %copy-start.4 = (bf16[1,128,256]{2,1,0:T(8,128)(2,1)S(1)}, bf16[1,128,256]{2,1,0:T(8,128)(2,1)}, u32[]{:S(2)}) copy-start(bf16[1,128,256]{2,1,0:T(8,128)(2,1)} %param.7) | copy-start | bytes 196612
  80.7 1.2 copy-start.1
  92.6 18.3 %collective-permute-start = (bf16[2048,128]{1,0:T(8,128)(2,1)S(1)}, bf16[2048,128]{1,0:T(8,128)(2,1)S(1)}, u32[]{:S(2)}, u32[]{:S(2)}) collective-permute-start(bf16[2048,128]{1,0:T(8,128)(2,1)S(1)} %get-tuple-element.11), channel_id=1, source_target_pairs={{0,1},{1,0},{2,3},{3,2},{4,5},{5,4},{6,7},{7,6},{8,9},{9,8},{10,11... | collective-permute-start | bytes 1572872 | tf_op jit(solution)/shard_map/ppermute | solution.py:185
Sparse Core Ops, SparseCore 0:
  47.0 33.6 all-gather.1

commit v2 on v1

--- a/solution.py
+++ b/solution.py
@@ -14,7 +14,8 @@
 BP = 256
 NEG = -1e30
 DP = ("x", "y", "c")
-CTX = ("zh", "zl")
+QUAD = ("zm", "zl")
+CTX = ("zh",) + QUAD
 F32 = jnp.float32
 BF16 = jnp.bfloat16
 
@@ -28,16 +29,17 @@
 
 
 def grads_kernel(
-    info, q_ref, do_ref, bkv_ref, kv_ref,
+    info, q_ref, do_ref, bkv_ref, near_ref, far_ref,
     dq_ref, bg_ref, send_ref, keep_ref, bias_ref,
-    qs, dos, qt, dot_, e_s, d_s, m_s, l_s, w_s, f_s, acc,
+    qs, dos, qt, dot_, e_s, d_s, m_s, l_s, w_s, f_s, acc, kv_s,
 ):
     heads = q_ref.shape[1] // 128
     nb = q_ref.shape[0] // BLK
     wide = heads * BLK
     rows = nb * wide
-    total = kv_ref.shape[1]
+    total = near_ref.shape[0] + far_ref.shape[0]
     nblk = total // BP
+    even = info[nb] == 0
     scale = 128 ** -0.5
     c = scale * math.log2(math.e)
     for b in range(nb):
@@ -45,13 +47,25 @@
             at = (b * heads + h) * BLK
             qs[at:at + BLK, :] = q_ref[b * BLK:(b + 1) * BLK, h * 128:(h + 1) * 128]
             dos[at:at + BLK, :] = do_ref[b * BLK:(b + 1) * BLK, h * 128:(h + 1) * 128]
+    chunk = near_ref.shape[0]
+    quad = chunk // KBLK
+    apart = far_ref.shape[0] // chunk
+    for i in range(apart + 1):
+        home = lax.rem(info[nb + 1] + i, apart + 1) * chunk
+        for j in range(quad):
+            at = pl.multiple_of(home + j * KBLK, KBLK)
+            if i == 0:
+                kv_s[pl.ds(at, KBLK), :] = near_ref[j * KBLK:(j + 1) * KBLK, :]
+            else:
+                src = (j * apart + i - 1) * KBLK
+                kv_s[pl.ds(at, KBLK), :] = far_ref[src:src + KBLK, :]
     qt[...] = turn(qs[...])
     dot_[...] = turn(dos[...])
 
     def first(blk, carry):
         at = pl.multiple_of(blk * BP, BP)
-        k = kv_ref[0, pl.ds(at, BP), :]
-        v = kv_ref[1, pl.ds(at, BP), :]
+        k = kv_s[pl.ds(at, BP), :128]
+        v = kv_s[pl.ds(at, BP), 128:]
         pos = blk * BP + lax.broadcasted_iota(jnp.int32, (BP, wide), 0)
         for b in range(nb):
             cols = slice(b * wide, (b + 1) * wide)
@@ -101,7 +115,6 @@
         acc[:, cols] = mm(turn(bk), ds)
 
     delta = f_s[nblk:nblk + 1, :]
-    even = info[nb] == 0
 
     def second(blk, carry):
         sum_k, sum_v = carry
@@ -111,9 +124,11 @@
         p = p.astype(BF16)
         dk = mm(ds, qs[...]) * scale
         dv = mm(p, dos[...])
-        acc[...] += mm(turn(kv_ref[0, pl.ds(at, BP), :]), ds)
-        keep_ref[pl.ds(at, BP), :] = jnp.where(even, dk, dv)
-        send_ref[pl.ds(at, BP), :] = jnp.where(even, dv, dk).astype(BF16)
+        acc[...] += mm(turn(kv_s[pl.ds(at, BP), :128]), ds)
+        to = pl.multiple_of(blk * KBLK, KBLK)
+        for x, cols in ((dk, slice(0, 128)), (dv, slice(128, 256))):
+            keep_ref[pl.ds(to, KBLK), cols] = jnp.where(even, x[:KBLK], x[KBLK:])
+            send_ref[pl.ds(to, KBLK), cols] = jnp.where(even, x[KBLK:], x[:KBLK]).astype(BF16)
         return (sum_k + dk.sum(0, keepdims=True), sum_v + dv.sum(0, keepdims=True))
 
     start = (sum(o[0] for o in own), sum(o[1] for o in own))
@@ -132,9 +147,9 @@
         bias_ref[h:h + 1, :] = part
 
 
-def grads(info, q, do, bkv, kv):
+def grads(info, q, do, bkv, near, far):
     rows, width = q.shape
-    total = kv.shape[1]
+    total = near.shape[0] + far.shape[0]
     wide = rows * width // 128
     nblk = total // BP
     vmem = pl.BlockSpec(memory_space=pltpu.VMEM)
@@ -143,11 +158,11 @@
         out_shape=(
             jax.ShapeDtypeStruct((rows, width), BF16),
             jax.ShapeDtypeStruct((rows, 256), BF16),
-            jax.ShapeDtypeStruct((total, 128), BF16),
-            jax.ShapeDtypeStruct((total, 128), F32),
+            jax.ShapeDtypeStruct((total // 2, 256), BF16),
+            jax.ShapeDtypeStruct((total // 2, 256), F32),
             jax.ShapeDtypeStruct((16, 128), F32),
         ),
-        in_specs=[pl.BlockSpec(memory_space=pltpu.SMEM)] + [vmem] * 4,
+        in_specs=[pl.BlockSpec(memory_space=pltpu.SMEM)] + [vmem] * 5,
         out_specs=(vmem,) * 5,
         scratch_shapes=[
             pltpu.VMEM((wide, 128), BF16),
@@ -161,49 +176,60 @@
             pltpu.VMEM((nblk, wide), F32),
             pltpu.VMEM((nblk + 8, wide), F32),
             pltpu.VMEM((128, wide), F32),
+            pltpu.VMEM((total, 256), BF16),
         ],
         compiler_params=pltpu.CompilerParams(vmem_limit_bytes=40 * 2**20),
         cost_estimate=pl.CostEstimate(
             flops=10 * wide * total * 128, bytes_accessed=3 * 2**20, transcendentals=wide * total
         ),
-    )(info, q, do, bkv, kv)
+    )(info, q, do, bkv, near, far)
+
+
+SWAP = [(0, 1), (1, 0)]
 
 
 def body(prompt_kv, queries, branch_kv, dout, prefix):
-    n = lax.axis_size(CTX)
-    place = lax.axis_index(CTX)
+    n = lax.axis_size("zh")
+    zh, zm, zl = (lax.axis_index(a) for a in CTX)
     rows = queries.shape[1]
     nb = rows // BLK
     keys = prompt_kv.shape[1]
-    halves = prompt_kv[0].reshape(keys, 2, 128).transpose(1, 0, 2)
-    out = jnp.broadcast_to(halves[None], (n // 2, 2, keys, 128)).reshape(n, keys, 128)
-    mine = lax.all_to_all(out, CTX, 0, 0, tiled=True).reshape(1, n * keys, 128)
-    kv = lax.all_gather(mine, "zl", axis=0, tiled=True)
-    mine_prefix = lax.dynamic_slice_in_dim(prefix[0], place * nb, nb)
-    info = jnp.concatenate([mine_prefix, lax.axis_index("zl").reshape(1)])
-    dq, bg, send, keep, bias = grads(info, queries[0], dout[0], branch_kv[0], kv)
-    got = lax.ppermute(send, "zl", [(0, 1), (1, 0)])
+    mine = prompt_kv[0]
+    near = lax.all_to_all(jnp.broadcast_to(mine[None], (4, keys, 256)), QUAD, 0, 0, tiled=True)
+    column = lax.all_gather(mine, "zh")
+    others = lax.dynamic_slice_in_dim(jnp.concatenate([column, column]), zh + 1, n - 1)
+    far = lax.all_gather(others.reshape(-1, 256), QUAD, axis=0, tiled=True)
+    mine_prefix = lax.dynamic_slice_in_dim(prefix[0], lax.axis_index(CTX) * nb, nb)
+    info = jnp.concatenate([mine_prefix, jnp.stack([zl, zh])])
+    dq, bg, send, keep, bias = grads(
+        info, queries[0], dout[0], branch_kv[0], near.reshape(-1, 256), far
+    )
+    got = lax.ppermute(send, "zl", SWAP)
     bias = lax.psum(bias, "c")
     flat = lax.axis_size(("x", "y"))
     bias = lax.all_to_all(
         jnp.broadcast_to(bias[None], (flat, 16, 128)), ("x", "y"), 0, 0, tiled=True
     ).sum(0)
+    pair = (keep + got.astype(F32)).reshape(n, 2, keys, 256)
+    away = lax.dynamic_index_in_dim(pair, 1 - zm, 1, keepdims=False).astype(BF16)
+    home = lax.dynamic_index_in_dim(pair, zm, 1, keepdims=False)
+    away, bias = lax.optimization_barrier((away, bias))
+    got = lax.ppermute(away, "zm", SWAP)
+    bias = lax.psum(bias, QUAD)
     high = bias.astype(BF16)
     low = (bias - high.astype(F32)).astype(BF16)
-    extra = jnp.concatenate([high, low], 0)
-    pair = (keep + got.astype(F32)).astype(BF16).reshape(n, keys, 128)
-    parcel = jnp.concatenate([pair, jnp.broadcast_to(extra[None], (n, 32, 128))], 1)
-    parcel = lax.all_to_all(parcel, CTX, 0, 0, tiled=True).astype(F32)
-    sums = parcel.reshape(n // 2, 2, keys + 32, 128).sum(0)
-    kv_grad = jnp.concatenate([sums[0, :keys], sums[1, :keys]], 1)
-    bias = sums[:, keys:].sum(0)
-    bias = (bias[:10] + bias[16:26]).reshape(-1)
-    return dq[None], kv_grad[None].astype(BF16), bg[None], bias
+    extra = jnp.concatenate([high, low], 1)
+    parcel = (home + got.astype(F32)).astype(BF16)
+    parcel = jnp.concatenate([parcel, jnp.broadcast_to(extra[None], (n, 16, 256))], 1)
+    sums = lax.all_to_all(parcel, "zh", 0, 0, tiled=True).astype(F32).sum(0)
+    bias = (sums[keys:, :128] + sums[keys:, 128:])[:10].reshape(-1)
+    return dq[None], sums[None, :keys].astype(BF16), bg[None], bias
 
 
 def solution(mesh):
     fine = Mesh(
-        mesh.devices.reshape(4, 4, 2, mesh.shape["ctx"] // 2, 2), ("x", "y", "c", "zh", "zl")
+        mesh.devices.reshape(4, 4, 2, mesh.shape["ctx"] // 4, 2, 2),
+        ("x", "y", "c", "zh", "zm", "zl"),
     )
     split = P(DP, CTX, None)
     return jax.shard_map(

time: 167 us -> 131 us (0.78)
  the two profiles are of different devices: /device:TPU:1 before, /device:TPU:64 now
where the time goes in v2:
time: 131 us
  blocking collectives  85.5 us (65%)
  starting transfers between devices  21.7 us (17%)
  Pallas kernels  10.6 us (8%)
  waiting for transfers between devices  7.85 us (6%)
  local copies, waits for them, and re-layouts  3.01 us (2%)
    all_to_all x1, blocking collectives, body(): sums = lax.all_to_all(parcel, 'zh', 0, 0, tiled=True).astype(F32).sum(0)  26.7 us
    all_gather x1, blocking collectives, body(): column = lax.all_gather(mine, 'zh')  25.7 us
    all_gather x1, blocking collectives, body(): far = lax.all_gather(others.reshape(-1, 256), QUAD, axis=0, tiled=True)  15.9 us
    psum x1, blocking collectives, body(): bias = lax.psum(bias, QUAD)  14.7 us
    pallas_call x1, Pallas kernels, grads(): pl.pallas_call(grads_kernel, out_shape=(jax.ShapeDtypeStruct((rows, width...  10.6 us
    all_to_all x1, starting transfers between devices, body(): lax.all_to_all(jnp.broadcast_to(mine[None], (4, keys, 256)), QUAD, 0, 0,...  8.54 us
    all_to_all x1, waiting for transfers between devices, body(): lax.all_to_all(jnp.broadcast_to(bias[None], (flat, 16, 128)), ('x', 'y'),...  7.84 us
    all_to_all x1, starting transfers between devices, body(): lax.all_to_all(jnp.broadcast_to(bias[None], (flat, 16, 128)), ('x', 'y'),...  7.04 us
  transfers between devices with their start and end apart: 4, of which 1 were waited for; matrix products, arithmetic and copies ran while one was open for 1% of the time, Pallas kernels for 0%

profile of v2, /device:TPU:64, one launch (start us, length us, event | category | flops | bytes accessed | tf_op | source)
XLA Modules:
  0.0 130.6 jit_solution(14995994666912113486)
XLA Ops:
  0.6 0.0 copy-start
  0.6 1.6 %broadcast_in_dim.13 = bf16[4,128,256]{2,1,0:T(8,128)(2,1)} broadcast(bf16[128,256]{1,0:T(8,128)(2,1)} %bitcast.30), dimensions={1,2} | broadcast | bytes 327680 | tf_op jit(solution)/shard_map/broadcast_in_dim | solution.py:198
  2.2 8.5 %all-to-all-start = ((bf16[4,128,256]{2,1,0:T(8,128)(2,1)}), bf16[4,128,256]{2,1,0:T(8,128)(2,1)S(1)}, u32[]{:S(2)}, u32[]{:S(2)}) async-start(bf16[4,128,256]{2,1,0:T(8,128)(2,1)} %broadcast_in_dim.13), calls=%async_computation | async-start | bytes 524288 | tf_op jit(solution)/shard_map/all_to_all | solution.py:198
  10.8 25.7 %all_gather.6 = bf16[4,128,256]{2,1,0:T(8,128)(2,1)S(1)} all-gather(bf16[1,128,256]{2,1,0:T(8,128)(2,1)S(1)} %copy-done.4), channel_id=1, replica_groups=mesh['x'=4,'y'=4,'c'=2,'zh'=4,'zm'=2,'zl'=2] {'zh'}, dimensions={0}, use_global_device_ids=true | all-gather | bytes 327680 | tf_op jit(solution)/shard_map/all_gather | solution.py:199
  36.4 0.1 fusion.5
  36.5 0.1 pad_add_fusion.info
  36.6 0.1 fusion.2
  36.7 0.0 copy-start.1
  36.7 0.0 copy-start.2
  36.7 0.0 copy-start.3
  36.7 15.9 %all_gather.7.far_ref = bf16[1536,256]{1,0:T(8,128)(2,1)S(1)} all-gather(bf16[384,256]{1,0:T(8,128)(2,1)S(1)} %bitcast.29), channel_id=1, replica_groups=mesh['x'=4,'y'=4,'c'=2,'zh'=4,'zm'=2,'zl'=2] {'zm','zl'}, dimensions={0}, use_global_device_ids=true | all-gather | bytes 983040 | tf_op jit(solution)/shard_map/all_gather | solution.py:201
  52.6 10.6 %shard_map.84 = (bf16[128,1024]{1,0:T(8,128)(2,1)}, bf16[128,256]{1,0:T(8,128)(2,1)}, bf16[1024,256]{1,0:T(8,128)(2,1)S(1)}, f32[1024,256]{1,0:T(8,128)S(1)}, f32[16,128]{1,0:T(8,128)S(1)}) custom-call(s32[4]{0:T(128)S(1)} %pad_add_fusion.info, bf16[128,1024]{1,0:T(8,128)(2,1)S(1)} %bitcast.24, bf16[128,1024]{1,0:T(8,128)(2,1)S(1)} %bitcast.25, ...), custom_call_target="tpu_custom_call" | custom-call | flops 2684354560 | bytes 3145728 | tf_op jit(solution)/shard_map/pallas_call | solution.py:156
  63.2 4.0 %collective-permute-start = (bf16[1024,256]{1,0:T(8,128)(2,1)S(1)}, bf16[1024,256]{1,0:T(8,128)(2,1)S(1)}, u32[]{:S(2)}, u32[]{:S(2)}) collective-permute-start(bf16[1024,256]{1,0:T(8,128)(2,1)S(1)} %get-tuple-element.13), channel_id=1, source_target_pairs={{0,1},{1,0},{2,3},{3,2},{4,5},{5,4},{6,7},{7,6},{8,9},{9,8},{10,11... | collective-permute-start | bytes 1572872 | tf_op jit(solution)/shard_map/ppermute | solution.py:207
  67.2 2.5 %psum.14 = f32[16,128]{1,0:T(8,128)S(1)} all-reduce(f32[16,128]{1,0:T(8,128)S(1)} %get-tuple-element.14), channel_id=1, replica_groups=mesh['x'=4,'y'=4,'c'=2,'zh'=4,'zm'=2,'zl'=2] {'c'}, use_global_device_ids=true, to_apply=%region_0.0 | all-reduce | flops 2048 | bytes 16384 | tf_op jit(solution)/shard_map/psum | solution.py:208
  69.7 0.7 broadcast_in_dim.29
  70.3 7.0 %all-to-all-start.1 = ((f32[16,16,128]{2,1,0:T(8,128)}), f32[16,16,128]{2,1,0:T(8,128)S(1)}, u32[]{:S(2)}, u32[]{:S(2)}) async-start(f32[16,16,128]{2,1,0:T(8,128)} %broadcast_in_dim.29), calls=%async_computation.1 | async-start | bytes 262144 | tf_op jit(solution)/shard_map/all_to_all | solution.py:210
  77.4 7.8 %all-to-all-done.1 = f32[16,16,128]{2,1,0:T(8,128)S(1)} async-done(((f32[16,16,128]{2,1,0:T(8,128)}), f32[16,16,128]{2,1,0:T(8,128)S(1)}, u32[]{:S(2)}, u32[]{:S(2)}) %all-to-all-start.1) | async-done | bytes 131104 | tf_op jit(solution)/shard_map/all_to_all | solution.py:210
  85.2 0.1 convert_add_fusion
  85.4 2.2 %collective-permute-start.1 = (bf16[4,128,256]{2,1,0:T(8,128)(2,1)S(1)}, bf16[4,128,256]{2,1,0:T(8,128)(2,1)S(1)}, u32[]{:S(2)}, u32[]{:S(2)}) collective-permute-start(bf16[4,128,256]{2,1,0:T(8,128)(2,1)S(1)} %fusion.1), channel_id=1, source_target_pairs={{0,2},{2,0},{1,3},{3,1},{4,6},{6,4},{5,7},{7,5},{8,10},{10,8},{9,1... | collective-permute-start | bytes 786440 | tf_op jit(solution)/shard_map/ppermute | solution.py:217
  87.6 14.7 %psum.15 = f32[16,128]{1,0:T(8,128)S(1)} all-reduce(f32[16,128]{1,0:T(8,128)S(1)} %reduce_sum.18), channel_id=1, replica_groups=mesh['x'=4,'y'=4,'c'=2,'zh'=4,'zm'=2,'zl'=2] {'zm','zl'}, use_global_device_ids=true, to_apply=%region_2.3 | all-reduce | flops 2048 | bytes 16384 | tf_op jit(solution)/shard_map/psum | solution.py:218
  102.4 0.1 fusion
  102.5 26.7 %all_to_all.15 = bf16[4,144,256]{2,1,0:T(8,128)(2,1)S(1)} all-to-all(bf16[4,144,256]{2,1,0:T(8,128)(2,1)S(1)} %pad_maximum_fusion), channel_id=1, replica_groups=mesh['x'=4,'y'=4,'c'=2,'zh'=4,'zm'=2,'zl'=2] {'zh'}, dimensions={0} | all-to-all | bytes 589824 | tf_op jit(solution)/shard_map/all_to_all | solution.py:224
  129.3 0.6 fusion.3
  130.0 0.6 fusion.4
  (17 shorter events, 0.2 us)
Async XLA Ops:
  0.6 35.8 %copy-start = (s32[1,32]{1,0:T(1,128)S(1)}, s32[1,32]{1,0:T(1,128)}, u32[]{:S(2)}) copy-start(s32[1,32]{1,0:T(1,128)} %param.9) | copy-start | bytes 388
  2.2 8.5 %copy-start.4 = (bf16[1,128,256]{2,1,0:T(8,128)(2,1)S(1)}, bf16[1,128,256]{2,1,0:T(8,128)(2,1)}, u32[]{:S(2)}) copy-start(bf16[1,128,256]{2,1,0:T(8,128)(2,1)} %param.5) | copy-start | bytes 196612
  2.2 50.4 %all-to-all-start = ((bf16[4,128,256]{2,1,0:T(8,128)(2,1)}), bf16[4,128,256]{2,1,0:T(8,128)(2,1)S(1)}, u32[]{:S(2)}, u32[]{:S(2)}) async-start(bf16[4,128,256]{2,1,0:T(8,128)(2,1)} %broadcast_in_dim.13), calls=%async_computation | async-start | bytes 524288 | tf_op jit(solution)/shard_map/all_to_all | solution.py:198
  36.7 16.0 %copy-start.1 = (bf16[1,128,1024]{2,1,0:T(8,128)(2,1)S(1)}, bf16[1,128,1024]{2,1,0:T(8,128)(2,1)}, u32[]{:S(2)}) copy-start(bf16[1,128,1024]{2,1,0:T(8,128)(2,1)} %param.6) | copy-start | bytes 786436
  36.7 15.9 %copy-start.2 = (bf16[1,128,1024]{2,1,0:T(8,128)(2,1)S(1)}, bf16[1,128,1024]{2,1,0:T(8,128)(2,1)}, u32[]{:S(2)}) copy-start(bf16[1,128,1024]{2,1,0:T(8,128)(2,1)} %param.8) | copy-start | bytes 786436
  36.7 15.9 %copy-start.3 = (bf16[1,128,256]{2,1,0:T(8,128)(2,1)S(1)}, bf16[1,128,256]{2,1,0:T(8,128)(2,1)}, u32[]{:S(2)}) copy-start(bf16[1,128,256]{2,1,0:T(8,128)(2,1)} %param.7) | copy-start | bytes 196612
  63.2 22.0 %collective-permute-start = (bf16[1024,256]{1,0:T(8,128)(2,1)S(1)}, bf16[1024,256]{1,0:T(8,128)(2,1)S(1)}, u32[]{:S(2)}, u32[]{:S(2)}) collective-permute-start(bf16[1024,256]{1,0:T(8,128)(2,1)S(1)} %get-tuple-element.13), channel_id=1, source_target_pairs={{0,1},{1,0},{2,3},{3,2},{4,5},{5,4},{6,7},{7,6},{8,9},{9,8},{10,11... | collective-permute-start | bytes 1572872 | tf_op jit(solution)/shard_map/ppermute | solution.py:207
  70.3 14.9 %all-to-all-start.1 = ((f32[16,16,128]{2,1,0:T(8,128)}), f32[16,16,128]{2,1,0:T(8,128)S(1)}, u32[]{:S(2)}, u32[]{:S(2)}) async-start(f32[16,16,128]{2,1,0:T(8,128)} %broadcast_in_dim.29), calls=%async_computation.1 | async-start | bytes 262144 | tf_op jit(solution)/shard_map/all_to_all | solution.py:210
  85.4 17.0 %collective-permute-start.1 = (bf16[4,128,256]{2,1,0:T(8,128)(2,1)S(1)}, bf16[4,128,256]{2,1,0:T(8,128)(2,1)S(1)}, u32[]{:S(2)}, u32[]{:S(2)}) collective-permute-start(bf16[4,128,256]{2,1,0:T(8,128)(2,1)S(1)} %fusion.1), channel_id=1, source_target_pairs={{0,2},{2,0},{1,3},{3,1},{4,6},{6,4},{5,7},{7,5},{8,10},{10,8},{9,1... | collective-permute-start | bytes 786440 | tf_op jit(solution)/shard_map/ppermute | solution.py:217

commit v3 on v2

--- a/solution.py
+++ b/solution.py
@@ -11,7 +11,7 @@
 
 BLK = 64
 KBLK = 128
-BP = 256
+BP = 512
 NEG = -1e30
 DP = ("x", "y", "c")
 QUAD = ("zm", "zl")
@@ -24,6 +24,10 @@
     return jnp.dot(a, b, preferred_element_type=F32)
 
 
+def nt(a, b):
+    return lax.dot_general(a, b, (((1,), (1,)), ((), ())), preferred_element_type=F32)
+
+
 def turn(a):
     return a.astype(F32).T.astype(BF16)
 
@@ -31,7 +35,7 @@
 def grads_kernel(
     info, q_ref, do_ref, bkv_ref, near_ref, far_ref,
     dq_ref, bg_ref, send_ref, keep_ref, bias_ref,
-    qs, dos, qt, dot_, e_s, d_s, m_s, l_s, w_s, f_s, acc, kv_s,
+    qs, dos, e_s, d_s, m_s, l_s, w_s, f_s, acc, kv_s,
 ):
     heads = q_ref.shape[1] // 128
     nb = q_ref.shape[0] // BLK
@@ -39,6 +43,7 @@
     rows = nb * wide
     total = near_ref.shape[0] + far_ref.shape[0]
     nblk = total // BP
+    units = total // KBLK
     even = info[nb] == 0
     scale = 128 ** -0.5
     c = scale * math.log2(math.e)
@@ -59,29 +64,28 @@
             else:
                 src = (j * apart + i - 1) * KBLK
                 kv_s[pl.ds(at, KBLK), :] = far_ref[src:src + KBLK, :]
-    qt[...] = turn(qs[...])
-    dot_[...] = turn(dos[...])
 
     def first(blk, carry):
         at = pl.multiple_of(blk * BP, BP)
         k = kv_s[pl.ds(at, BP), :128]
         v = kv_s[pl.ds(at, BP), 128:]
-        pos = blk * BP + lax.broadcasted_iota(jnp.int32, (BP, wide), 0)
         for b in range(nb):
             cols = slice(b * wide, (b + 1) * wide)
-            s = mm(k, qt[:, cols]) * c
-            s = jnp.where(pos < info[b] * KBLK, s, NEG)
-            m = s.max(0, keepdims=True)
-            e = jnp.exp2(s - m)
-            d = mm(v, dot_[:, cols])
-            e_s[pl.ds(at, BP), cols] = e
+            s = nt(k, qs[cols, :])
+            d = nt(v, dos[cols, :])
             d_s[pl.ds(at, BP), cols] = d
-            m_s[pl.ds(blk, 1), cols] = m
-            l_s[pl.ds(blk, 1), cols] = e.sum(0, keepdims=True)
-            w_s[pl.ds(blk, 1), cols] = (e * d).sum(0, keepdims=True)
+            for u in range(BP // KBLK):
+                unit = blk * (BP // KBLK) + u
+                su, du = s[u * KBLK:(u + 1) * KBLK], d[u * KBLK:(u + 1) * KBLK]
+                m = su.max(0, keepdims=True)
+                e = jnp.exp2((su - m) * c)
+                e_s[pl.ds(at + u * KBLK, KBLK), cols] = e
+                m_s[pl.ds(unit, 1), cols] = jnp.where(unit < info[b], m * c, NEG)
+                l_s[pl.ds(unit, 1), cols] = e.sum(0, keepdims=True)
+                w_s[pl.ds(unit, 1), cols] = (e * du).sum(0, keepdims=True)
         return carry
 
-    lax.fori_loop(0, nblk, first, 0)
+    lax.fori_loop(0, nblk, first, 0, unroll=4)
 
     own = []
     row_in = lax.broadcasted_iota(jnp.int32, (BLK, wide), 1) % BLK
@@ -91,10 +95,10 @@
         cols = slice(b * wide, (b + 1) * wide)
         bk = bkv_ref[b * BLK:(b + 1) * BLK, :128]
         bv = bkv_ref[b * BLK:(b + 1) * BLK, 128:]
-        s = jnp.where(causal, mm(bk, qt[:, cols]) * c, NEG)
+        s = jnp.where(causal, nt(bk, qs[cols, :]) * c, NEG)
         m = s.max(0, keepdims=True)
         e = jnp.exp2(s - m)
-        d = mm(bv, dot_[:, cols])
+        d = nt(bv, dos[cols, :])
         top = jnp.maximum(m, m_s[:, cols].max(0, keepdims=True))
         scales = jnp.exp2(m_s[:, cols] - top)
         mine = jnp.exp2(m - top)
@@ -102,8 +106,8 @@
         dots = (w_s[:, cols] * scales).sum(0, keepdims=True) + (e * d).sum(0, keepdims=True) * mine
         inv = 1.0 / mass
         delta = dots * inv
-        f_s[:nblk, cols] = scales * inv
-        f_s[nblk:nblk + 1, cols] = delta
+        f_s[:units, cols] = scales * inv
+        f_s[units:units + 1, cols] = delta
         p = e * (mine * inv)
         ds = (p * (d - delta)).astype(BF16)
         p = p.astype(BF16)
@@ -114,28 +118,31 @@
         own.append((own_k.sum(0, keepdims=True), own_v.sum(0, keepdims=True)))
         acc[:, cols] = mm(turn(bk), ds)
 
-    delta = f_s[nblk:nblk + 1, :]
+    delta = f_s[units:units + 1, :]
 
     def second(blk, carry):
         sum_k, sum_v = carry
         at = pl.multiple_of(blk * BP, BP)
-        p = e_s[pl.ds(at, BP), :] * f_s[pl.ds(blk, 1), :]
+        p = jnp.concatenate([
+            e_s[pl.ds(at + u * KBLK, KBLK), :] * f_s[pl.ds(blk * (BP // KBLK) + u, 1), :]
+            for u in range(BP // KBLK)
+        ])
         ds = (p * (d_s[pl.ds(at, BP), :] - delta)).astype(BF16)
         p = p.astype(BF16)
         dk = mm(ds, qs[...]) * scale
         dv = mm(p, dos[...])
         acc[...] += mm(turn(kv_s[pl.ds(at, BP), :128]), ds)
-        to = pl.multiple_of(blk * KBLK, KBLK)
-        for x, cols in ((dk, slice(0, 128)), (dv, slice(128, 256))):
-            keep_ref[pl.ds(to, KBLK), cols] = jnp.where(even, x[:KBLK], x[KBLK:])
-            send_ref[pl.ds(to, KBLK), cols] = jnp.where(even, x[KBLK:], x[:KBLK]).astype(BF16)
+        for u in range(0, BP // KBLK, 2):
+            to = pl.multiple_of(blk * (BP // 2) + u * (KBLK // 2), KBLK)
+            for x, cols in ((dk, slice(0, 128)), (dv, slice(128, 256))):
+                x0, x1 = x[u * KBLK:(u + 1) * KBLK], x[(u + 1) * KBLK:(u + 2) * KBLK]
+                keep_ref[pl.ds(to, KBLK), cols] = jnp.where(even, x0, x1)
+                send_ref[pl.ds(to, KBLK), cols] = jnp.where(even, x1, x0).astype(BF16)
         return (sum_k + dk.sum(0, keepdims=True), sum_v + dv.sum(0, keepdims=True))
 
     start = (sum(o[0] for o in own), sum(o[1] for o in own))
-    sum_k, sum_v = lax.fori_loop(0, nblk, second, start)
-    bias_ref[...] = jnp.zeros_like(bias_ref)
-    bias_ref[heads:heads + 1, :] = sum_k
-    bias_ref[heads + 1:heads + 2, :] = sum_v
+    sum_k, sum_v = lax.fori_loop(0, nblk, second, start, unroll=4)
+    parts = []
     dq = acc[...].T * scale
     for h in range(heads):
         part = jnp.zeros((1, 128), F32)
@@ -144,14 +151,16 @@
             piece = dq[at:at + BLK, :]
             part += piece.sum(0, keepdims=True)
             dq_ref[b * BLK:(b + 1) * BLK, h * 128:(h + 1) * 128] = piece.astype(BF16)
-        bias_ref[h:h + 1, :] = part
-
-
-def grads(info, q, do, bkv, near, far):
+        parts.append(part)
+    parts += [sum_k, sum_v, jnp.zeros((14 - heads, 128), F32)]
+    bias_ref[...] = jnp.broadcast_to(jnp.concatenate(parts)[None], bias_ref.shape)
+
+
+def grads(info, q, do, bkv, near, far, copies):
     rows, width = q.shape
     total = near.shape[0] + far.shape[0]
     wide = rows * width // 128
-    nblk = total // BP
+    units = total // KBLK
     vmem = pl.BlockSpec(memory_space=pltpu.VMEM)
     return pl.pallas_call(
         grads_kernel,
@@ -160,21 +169,19 @@
             jax.ShapeDtypeStruct((rows, 256), BF16),
             jax.ShapeDtypeStruct((total // 2, 256), BF16),
             jax.ShapeDtypeStruct((total // 2, 256), F32),
-            jax.ShapeDtypeStruct((16, 128), F32),
+            jax.ShapeDtypeStruct((copies, 16, 128), F32),
         ),
         in_specs=[pl.BlockSpec(memory_space=pltpu.SMEM)] + [vmem] * 5,
         out_specs=(vmem,) * 5,
         scratch_shapes=[
             pltpu.VMEM((wide, 128), BF16),
             pltpu.VMEM((wide, 128), BF16),
-            pltpu.VMEM((128, wide), BF16),
-            pltpu.VMEM((128, wide), BF16),
             pltpu.VMEM((total, wide), F32),
             pltpu.VMEM((total, wide), F32),
-            pltpu.VMEM((nblk, wide), F32),
-            pltpu.VMEM((nblk, wide), F32),
-            pltpu.VMEM((nblk, wide), F32),
-            pltpu.VMEM((nblk + 8, wide), F32),
+            pltpu.VMEM((units, wide), F32),
+            pltpu.VMEM((units, wide), F32),
+            pltpu.VMEM((units, wide), F32),
+            pltpu.VMEM((units + 8, wide), F32),
             pltpu.VMEM((128, wide), F32),
             pltpu.VMEM((total, 256), BF16),
         ],
@@ -202,19 +209,16 @@
     mine_prefix = lax.dynamic_slice_in_dim(prefix[0], lax.axis_index(CTX) * nb, nb)
     info = jnp.concatenate([mine_prefix, jnp.stack([zl, zh])])
     dq, bg, send, keep, bias = grads(
-        info, queries[0], dout[0], branch_kv[0], near.reshape(-1, 256), far
+        info, queries[0], dout[0], branch_kv[0], near.reshape(-1, 256), far, lax.axis_size(DP)
     )
     got = lax.ppermute(send, "zl", SWAP)
-    bias = lax.psum(bias, "c")
-    flat = lax.axis_size(("x", "y"))
-    bias = lax.all_to_all(
-        jnp.broadcast_to(bias[None], (flat, 16, 128)), ("x", "y"), 0, 0, tiled=True
-    ).sum(0)
+    bias = lax.all_to_all(bias, DP, 0, 0, tiled=True)
     pair = (keep + got.astype(F32)).reshape(n, 2, keys, 256)
     away = lax.dynamic_index_in_dim(pair, 1 - zm, 1, keepdims=False).astype(BF16)
     home = lax.dynamic_index_in_dim(pair, zm, 1, keepdims=False)
-    away, bias = lax.optimization_barrier((away, bias))
     got = lax.ppermute(away, "zm", SWAP)
+    bias, away = lax.optimization_barrier((bias, away))
+    bias = bias.sum(0)
     bias = lax.psum(bias, QUAD)
     high = bias.astype(BF16)
     low = (bias - high.astype(F32)).astype(BF16)

time: 131 us -> 121 us (0.924)
  the two profiles are of different devices: /device:TPU:64 before, /device:TPU:2 now
where the time goes in v3:
time: 121 us; the launch traced here: 120 us
  blocking collectives  85.1 us (70%)
  starting transfers between devices  18.8 us (16%)
  Pallas kernels  7.76 us (6%)
  waiting for transfers between devices  4.53 us (4%)
  local copies, waits for them, and re-layouts  2.35 us (2%)
    all_to_all x1, blocking collectives, body(): sums = lax.all_to_all(parcel, 'zh', 0, 0, tiled=True).astype(F32).sum(0)  27.7 us
    all_gather x1, blocking collectives, body(): column = lax.all_gather(mine, 'zh')  24.3 us
    all_gather x1, blocking collectives, body(): far = lax.all_gather(others.reshape(-1, 256), QUAD, axis=0, tiled=True)  22.2 us
    psum x1, blocking collectives, body(): bias = lax.psum(bias, QUAD)  10.8 us
    pallas_call x1, Pallas kernels, grads(): pl.pallas_call(grads_kernel, out_shape=(jax.ShapeDtypeStruct((rows, width...  7.76 us
    all_to_all x1, starting transfers between devices, body(): bias = lax.all_to_all(bias, DP, 0, 0, tiled=True)  7.63 us
    all_to_all x1, starting transfers between devices, body(): lax.all_to_all(jnp.broadcast_to(mine[None], (4, keys, 256)), QUAD, 0, 0,...  6.03 us
    ppermute x1, starting transfers between devices, body(): got = lax.ppermute(away, 'zm', SWAP)  3 us
  transfers between devices with their start and end apart: 4, of which 2 were waited for; matrix products, arithmetic and copies ran while one was open for 0% of the time, Pallas kernels for 0%

profile of v3, /device:TPU:2, one launch (start us, length us, event | category | flops | bytes accessed | tf_op | source)
XLA Modules:
  0.0 120.4 jit_solution(2356585220754827641)
XLA Ops:
  0.6 0.0 copy-start
  0.6 1.6 %broadcast_in_dim.21 = bf16[4,128,256]{2,1,0:T(8,128)(2,1)} broadcast(bf16[128,256]{1,0:T(8,128)(2,1)} %bitcast.30), dimensions={1,2} | broadcast | bytes 327680 | tf_op jit(solution)/shard_map/broadcast_in_dim | solution.py:205
  2.2 6.0 %all-to-all-start = ((bf16[4,128,256]{2,1,0:T(8,128)(2,1)}), bf16[4,128,256]{2,1,0:T(8,128)(2,1)S(1)}, u32[]{:S(2)}, u32[]{:S(2)}) async-start(bf16[4,128,256]{2,1,0:T(8,128)(2,1)} %broadcast_in_dim.21), calls=%async_computation | async-start | bytes 524288 | tf_op jit(solution)/shard_map/all_to_all | solution.py:205
  8.2 24.3 %all_gather.6 = bf16[4,128,256]{2,1,0:T(8,128)(2,1)S(1)} all-gather(bf16[1,128,256]{2,1,0:T(8,128)(2,1)S(1)} %copy-done.4), channel_id=1, replica_groups=mesh['x'=4,'y'=4,'c'=2,'zh'=4,'zm'=2,'zl'=2] {'zh'}, dimensions={0}, use_global_device_ids=true | all-gather | bytes 327680 | tf_op jit(solution)/shard_map/all_gather | solution.py:206
  32.6 0.1 fusion.5
  32.6 0.1 pad_add_fusion.info
  32.7 0.1 fusion.2
  32.8 0.0 copy-start.1
  32.8 0.0 copy-start.2
  32.8 0.0 copy-start.3
  32.8 22.2 %all_gather.7.far_ref = bf16[1536,256]{1,0:T(8,128)(2,1)S(1)} all-gather(bf16[384,256]{1,0:T(8,128)(2,1)S(1)} %bitcast.29), channel_id=1, replica_groups=mesh['x'=4,'y'=4,'c'=2,'zh'=4,'zm'=2,'zl'=2] {'zm','zl'}, dimensions={0}, use_global_device_ids=true | all-gather | bytes 983040 | tf_op jit(solution)/shard_map/all_gather | solution.py:208
  55.1 7.8 %shard_map.84 = (bf16[128,1024]{1,0:T(8,128)(2,1)}, bf16[128,256]{1,0:T(8,128)(2,1)}, bf16[1024,256]{1,0:T(8,128)(2,1)S(1)}, f32[1024,256]{1,0:T(8,128)S(1)}, f32[32,16,128]{2,1,0:T(8,128)}) custom-call(s32[4]{0:T(128)S(1)} %pad_add_fusion.info, bf16[128,1024]{1,0:T(8,128)(2,1)S(1)} %bitcast.24, bf16[128,1024]{1,0:T(8,128)(2,1)S(1)} %bitcast.25, ...), custom_call_target="tpu_custom_call" | custom-call | flops 2684354560 | bytes 3145728 | tf_op jit(solution)/shard_map/pallas_call | solution.py:165
  62.8 2.2 %collective-permute-start = (bf16[1024,256]{1,0:T(8,128)(2,1)S(1)}, bf16[1024,256]{1,0:T(8,128)(2,1)S(1)}, u32[]{:S(2)}, u32[]{:S(2)}) collective-permute-start(bf16[1024,256]{1,0:T(8,128)(2,1)S(1)} %get-tuple-element.12), channel_id=1, source_target_pairs={{0,1},{1,0},{2,3},{3,2},{4,5},{5,4},{6,7},{7,6},{8,9},{9,8},{10,11... | collective-permute-start | bytes 1572872 | tf_op jit(solution)/shard_map/ppermute | solution.py:214
  65.0 7.6 %all-to-all-start.1 = ((f32[32,16,128]{2,1,0:T(8,128)}), f32[32,16,128]{2,1,0:T(8,128)S(1)}, u32[]{:S(2)}, u32[]{:S(2)}) async-start(f32[32,16,128]{2,1,0:T(8,128)} %get-tuple-element.13), calls=%async_computation.1 | async-start | bytes 524288 | tf_op jit(solution)/shard_map/all_to_all | solution.py:215
  72.7 1.5 %collective-permute-done = bf16[1024,256]{1,0:T(8,128)(2,1)S(1)} collective-permute-done((bf16[1024,256]{1,0:T(8,128)(2,1)S(1)}, bf16[1024,256]{1,0:T(8,128)(2,1)S(1)}, u32[]{:S(2)}, u32[]{:S(2)}) %collective-permute-start) | collective-permute-done | bytes 524320 | tf_op jit(solution)/shard_map/ppermute | solution.py:214
  74.2 0.1 convert_add_fusion
  74.4 3.0 %collective-permute-start.1 = (bf16[4,128,256]{2,1,0:T(8,128)(2,1)S(1)}, bf16[4,128,256]{2,1,0:T(8,128)(2,1)S(1)}, u32[]{:S(2)}, u32[]{:S(2)}) collective-permute-start(bf16[4,128,256]{2,1,0:T(8,128)(2,1)S(1)} %fusion.1), channel_id=1, source_target_pairs={{0,2},{2,0},{1,3},{3,1},{4,6},{6,4},{5,7},{7,5},{8,10},{10,8},{9,1... | collective-permute-start | bytes 786440 | tf_op jit(solution)/shard_map/ppermute | solution.py:219
  77.4 3.0 %all-to-all-done.1 = f32[32,16,128]{2,1,0:T(8,128)S(1)} async-done(((f32[32,16,128]{2,1,0:T(8,128)}), f32[32,16,128]{2,1,0:T(8,128)S(1)}, u32[]{:S(2)}, u32[]{:S(2)}) %all-to-all-start.1) | async-done | bytes 262176 | tf_op jit(solution)/shard_map/all_to_all | solution.py:215
  80.4 10.8 %psum.7 = f32[16,128]{1,0:T(8,128)S(1)} all-reduce(f32[16,128]{1,0:T(8,128)S(1)} %reduce_sum.18), channel_id=1, replica_groups=mesh['x'=4,'y'=4,'c'=2,'zh'=4,'zm'=2,'zl'=2] {'zm','zl'}, use_global_device_ids=true, to_apply=%region_1.2 | all-reduce | flops 2048 | bytes 16384 | tf_op jit(solution)/shard_map/psum | solution.py:222
  91.2 0.0 collective-permute-done.1
  91.2 0.1 fusion
  91.4 27.7 %all_to_all.15 = bf16[4,144,256]{2,1,0:T(8,128)(2,1)S(1)} all-to-all(bf16[4,144,256]{2,1,0:T(8,128)(2,1)S(1)} %pad_maximum_fusion), channel_id=1, replica_groups=mesh['x'=4,'y'=4,'c'=2,'zh'=4,'zm'=2,'zl'=2] {'zh'}, dimensions={0} | all-to-all | bytes 589824 | tf_op jit(solution)/shard_map/all_to_all | solution.py:228
  119.2 0.6 fusion.3
  119.8 0.6 fusion.4
  (15 shorter events, 0.2 us)
Async XLA Ops:
  0.6 31.9 %copy-start = (s32[1,32]{1,0:T(1,128)S(1)}, s32[1,32]{1,0:T(1,128)}, u32[]{:S(2)}) copy-start(s32[1,32]{1,0:T(1,128)} %param.9) | copy-start | bytes 388
  2.2 6.0 %copy-start.4 = (bf16[1,128,256]{2,1,0:T(8,128)(2,1)S(1)}, bf16[1,128,256]{2,1,0:T(8,128)(2,1)}, u32[]{:S(2)}) copy-start(bf16[1,128,256]{2,1,0:T(8,128)(2,1)} %param.5) | copy-start | bytes 196612
  2.2 52.8 %all-to-all-start = ((bf16[4,128,256]{2,1,0:T(8,128)(2,1)}), bf16[4,128,256]{2,1,0:T(8,128)(2,1)S(1)}, u32[]{:S(2)}, u32[]{:S(2)}) async-start(bf16[4,128,256]{2,1,0:T(8,128)(2,1)} %broadcast_in_dim.21), calls=%async_computation | async-start | bytes 524288 | tf_op jit(solution)/shard_map/all_to_all | solution.py:205
  32.8 22.3 %copy-start.1 = (bf16[1,128,1024]{2,1,0:T(8,128)(2,1)S(1)}, bf16[1,128,1024]{2,1,0:T(8,128)(2,1)}, u32[]{:S(2)}) copy-start(bf16[1,128,1024]{2,1,0:T(8,128)(2,1)} %param.6) | copy-start | bytes 786436
  32.8 22.2 %copy-start.2 = (bf16[1,128,1024]{2,1,0:T(8,128)(2,1)S(1)}, bf16[1,128,1024]{2,1,0:T(8,128)(2,1)}, u32[]{:S(2)}) copy-start(bf16[1,128,1024]{2,1,0:T(8,128)(2,1)} %param.8) | copy-start | bytes 786436
  32.8 22.2 %copy-start.3 = (bf16[1,128,256]{2,1,0:T(8,128)(2,1)S(1)}, bf16[1,128,256]{2,1,0:T(8,128)(2,1)}, u32[]{:S(2)}) copy-start(bf16[1,128,256]{2,1,0:T(8,128)(2,1)} %param.7) | copy-start | bytes 196612
  62.8 11.4 %collective-permute-start = (bf16[1024,256]{1,0:T(8,128)(2,1)S(1)}, bf16[1024,256]{1,0:T(8,128)(2,1)S(1)}, u32[]{:S(2)}, u32[]{:S(2)}) collective-permute-start(bf16[1024,256]{1,0:T(8,128)(2,1)S(1)} %get-tuple-element.12), channel_id=1, source_target_pairs={{0,1},{1,0},{2,3},{3,2},{4,5},{5,4},{6,7},{7,6},{8,9},{9,8},{10,11... | collective-permute-start | bytes 1572872 | tf_op jit(solution)/shard_map/ppermute | solution.py:214
  65.0 15.4 %all-to-all-start.1 = ((f32[32,16,128]{2,1,0:T(8,128)}), f32[32,16,128]{2,1,0:T(8,128)S(1)}, u32[]{:S(2)}, u32[]{:S(2)}) async-start(f32[32,16,128]{2,1,0:T(8,128)} %get-tuple-element.13), calls=%async_computation.1 | async-start | bytes 524288 | tf_op jit(solution)/shard_map/all_to_all | solution.py:215
  74.4 16.8 %collective-permute-start.1 = (bf16[4,128,256]{2,1,0:T(8,128)(2,1)S(1)}, bf16[4,128,256]{2,1,0:T(8,128)(2,1)S(1)}, u32[]{:S(2)}, u32[]{:S(2)}) collective-permute-start(bf16[4,128,256]{2,1,0:T(8,128)(2,1)S(1)} %fusion.1), channel_id=1, source_target_pairs={{0,2},{2,0},{1,3},{3,1},{4,6},{6,4},{5,7},{7,5},{8,10},{10,8},{9,1... | collective-permute-start | bytes 786440 | tf_op jit(solution)/shard_map/ppermute | solution.py:219

commit v4 on v3

--- a/solution.py
+++ b/solution.py
@@ -11,6 +11,7 @@
 
 BLK = 64
 KBLK = 128
+ORDER = (2, 1, 3)
 BP = 512
 NEG = -1e30
 DP = ("x", "y", "c")
@@ -202,8 +203,9 @@
     nb = rows // BLK
     keys = prompt_kv.shape[1]
     mine = prompt_kv[0]
+    column = lax.all_gather(mine, "zh")
+    mine, column = lax.optimization_barrier((mine, column))
     near = lax.all_to_all(jnp.broadcast_to(mine[None], (4, keys, 256)), QUAD, 0, 0, tiled=True)
-    column = lax.all_gather(mine, "zh")
     others = lax.dynamic_slice_in_dim(jnp.concatenate([column, column]), zh + 1, n - 1)
     far = lax.all_gather(others.reshape(-1, 256), QUAD, axis=0, tiled=True)
     mine_prefix = lax.dynamic_slice_in_dim(prefix[0], lax.axis_index(CTX) * nb, nb)
@@ -219,15 +221,21 @@
     got = lax.ppermute(away, "zm", SWAP)
     bias, away = lax.optimization_barrier((bias, away))
     bias = bias.sum(0)
-    bias = lax.psum(bias, QUAD)
+    bias = lax.psum(lax.psum(bias, "zl"), "zm")
     high = bias.astype(BF16)
     low = (bias - high.astype(F32)).astype(BF16)
     extra = jnp.concatenate([high, low], 1)
-    parcel = (home + got.astype(F32)).astype(BF16)
-    parcel = jnp.concatenate([parcel, jnp.broadcast_to(extra[None], (n, 16, 256))], 1)
-    sums = lax.all_to_all(parcel, "zh", 0, 0, tiled=True).astype(F32).sum(0)
-    bias = (sums[keys:, :128] + sums[keys:, 128:])[:10].reshape(-1)
-    return dq[None], sums[None, :keys].astype(BF16), bg[None], bias
+    parcel = home + got.astype(F32)
+    sums = lax.dynamic_index_in_dim(parcel, zh, 0, keepdims=False)
+    both = jnp.zeros((16, 256), F32)
+    for far in ORDER:
+        sent = lax.dynamic_index_in_dim(parcel, (zh + far) % n, 0, keepdims=False)
+        sent = jnp.concatenate([sent.astype(BF16), extra])
+        came = lax.ppermute(sent, "zh", [(p, (p + far) % n) for p in range(n)]).astype(F32)
+        sums += came[:keys]
+        both += came[keys:]
+    bias = (bias + both[:, :128] + both[:, 128:])[:10].reshape(-1)
+    return dq[None], sums[None].astype(BF16), bg[None], bias
 
 
 def solution(mesh):

time: 121 us -> 121 us (level)
  the two profiles are of different devices: /device:TPU:2 before, /device:TPU:1 now
where the time goes in v4:
time: 121 us
  blocking collectives  56.3 us (47%)
  starting transfers between devices  39.5 us (33%)
  waiting for transfers between devices  13.9 us (11%)
  Pallas kernels  7.78 us (6%)
  other arithmetic  1.72 us (1%)
    all_gather x1, blocking collectives, body(): column = lax.all_gather(mine, 'zh')  25.6 us
    all_gather x1, blocking collectives, body(): far = lax.all_gather(others.reshape(-1, 256), QUAD, axis=0, tiled=True)  17.9 us
    ppermute x3, starting transfers between devices, body(): lax.ppermute(sent, 'zh', [(p, (p + far) % n) for p in range(n)]).astype(F32)  16.2 us
    all_to_all x1, starting transfers between devices, body(): bias = lax.all_to_all(bias, DP, 0, 0, tiled=True)  12.9 us
    psum x2, blocking collectives, body(): bias = lax.psum(lax.psum(bias, 'zl'), 'zm')  12.8 us
    ppermute x3, waiting for transfers between devices, body(): lax.ppermute(sent, 'zh', [(p, (p + far) % n) for p in range(n)]).astype(F32)  9.36 us
    pallas_call x1, Pallas kernels, grads(): pl.pallas_call(grads_kernel, out_shape=(jax.ShapeDtypeStruct((rows, width...  7.78 us
    all_to_all x1, waiting for transfers between devices, body(): bias = lax.all_to_all(bias, DP, 0, 0, tiled=True)  4.49 us
  transfers between devices with their start and end apart: 7, of which 3 were waited for; matrix products, arithmetic and copies ran while one was open for 0% of the time, Pallas kernels for 0%

profile of v4, /device:TPU:1, one launch (start us, length us, event | category | flops | bytes accessed | tf_op | source)
XLA Modules:
  0.0 120.9 jit_solution(15159104172828542112)
XLA Ops:
  0.6 0.0 copy-start
  0.7 25.6 %all_gather.6 = bf16[4,128,256]{2,1,0:T(8,128)(2,1)S(1)} all-gather(bf16[1,128,256]{2,1,0:T(8,128)(2,1)} %param.5), channel_id=1, replica_groups=mesh['x'=4,'y'=4,'c'=2,'zh'=4,'zm'=2,'zl'=2] {'zh'}, dimensions={0}, use_global_device_ids=true | all-gather | bytes 327680 | tf_op jit(solution)/shard_map/all_gather | solution.py:206
  26.3 0.7 broadcast_in_dim.6
  27.0 3.4 %all-to-all-start = ((bf16[4,128,256]{2,1,0:T(8,128)(2,1)}), bf16[4,128,256]{2,1,0:T(8,128)(2,1)S(1)}, u32[]{:S(2)}, u32[]{:S(2)}) async-start(bf16[4,128,256]{2,1,0:T(8,128)(2,1)} %broadcast_in_dim.6), calls=%async_computation | async-start | bytes 524288 | tf_op jit(solution)/shard_map/all_to_all | solution.py:208
  30.4 0.1 fusion.11
  30.5 0.1 pad_add_fusion.info
  30.6 0.1 fusion.1
  30.7 17.9 %all_gather.7.far_ref = bf16[1536,256]{1,0:T(8,128)(2,1)S(1)} all-gather(bf16[384,256]{1,0:T(8,128)(2,1)S(1)} %bitcast.41), channel_id=1, replica_groups=mesh['x'=4,'y'=4,'c'=2,'zh'=4,'zm'=2,'zl'=2] {'zm','zl'}, dimensions={0}, use_global_device_ids=true | all-gather | bytes 983040 | tf_op jit(solution)/shard_map/all_gather | solution.py:210
  48.6 7.8 %shard_map.84 = (bf16[128,1024]{1,0:T(8,128)(2,1)}, bf16[128,256]{1,0:T(8,128)(2,1)}, bf16[1024,256]{1,0:T(8,128)(2,1)S(1)}, f32[1024,256]{1,0:T(8,128)S(1)}, f32[32,16,128]{2,1,0:T(8,128)}) custom-call(s32[4]{0:T(128)S(1)} %pad_add_fusion.info, bf16[128,1024]{1,0:T(8,128)(2,1)S(1)} %bitcast.36, bf16[128,1024]{1,0:T(8,128)(2,1)S(1)} %bitcast.37, ...), custom_call_target="tpu_custom_call" | custom-call | flops 2684354560 | bytes 3145728 | tf_op jit(solution)/shard_map/pallas_call | solution.py:166
  56.4 2.7 %collective-permute-start = (bf16[1024,256]{1,0:T(8,128)(2,1)S(1)}, bf16[1024,256]{1,0:T(8,128)(2,1)S(1)}, u32[]{:S(2)}, u32[]{:S(2)}) collective-permute-start(bf16[1024,256]{1,0:T(8,128)(2,1)S(1)} %get-tuple-element.16), channel_id=1, source_target_pairs={{0,1},{1,0},{2,3},{3,2},{4,5},{5,4},{6,7},{7,6},{8,9},{9,8},{10,11... | collective-permute-start | bytes 1572872 | tf_op jit(solution)/shard_map/ppermute | solution.py:216
  59.2 12.9 %all-to-all-start.1 = ((f32[32,16,128]{2,1,0:T(8,128)}), f32[32,16,128]{2,1,0:T(8,128)S(1)}, u32[]{:S(2)}, u32[]{:S(2)}) async-start(f32[32,16,128]{2,1,0:T(8,128)} %get-tuple-element.17), calls=%async_computation.1 | async-start | bytes 524288 | tf_op jit(solution)/shard_map/all_to_all | solution.py:217
  72.1 0.1 convert_add_fusion
  72.3 4.3 %collective-permute-start.1 = (bf16[4,128,256]{2,1,0:T(8,128)(2,1)S(1)}, bf16[4,128,256]{2,1,0:T(8,128)(2,1)S(1)}, u32[]{:S(2)}, u32[]{:S(2)}) collective-permute-start(bf16[4,128,256]{2,1,0:T(8,128)(2,1)S(1)} %fusion), channel_id=1, source_target_pairs={{0,2},{2,0},{1,3},{3,1},{4,6},{6,4},{5,7},{7,5},{8,10},{10,8},{9,1... | collective-permute-start | bytes 786440 | tf_op jit(solution)/shard_map/ppermute | solution.py:221
  76.6 4.5 %all-to-all-done.1 = f32[32,16,128]{2,1,0:T(8,128)S(1)} async-done(((f32[32,16,128]{2,1,0:T(8,128)}), f32[32,16,128]{2,1,0:T(8,128)S(1)}, u32[]{:S(2)}, u32[]{:S(2)}) %all-to-all-start.1) | async-done | bytes 262176 | tf_op jit(solution)/shard_map/all_to_all | solution.py:217
  81.1 8.0 %psum.14 = f32[16,128]{1,0:T(8,128)S(1)} all-reduce(f32[16,128]{1,0:T(8,128)S(1)} %reduce_sum.9), channel_id=1, replica_groups=mesh['x'=4,'y'=4,'c'=2,'zh'=4,'zm'=2,'zl'=2] {'zl'}, use_global_device_ids=true, to_apply=%region_1.2 | all-reduce | flops 2048 | bytes 16384 | tf_op jit(solution)/shard_map/psum | solution.py:224
  89.1 4.7 %psum.15 = f32[16,128]{1,0:T(8,128)S(1)} all-reduce(f32[16,128]{1,0:T(8,128)S(1)} %psum.14), channel_id=1, replica_groups=mesh['x'=4,'y'=4,'c'=2,'zh'=4,'zm'=2,'zl'=2] {'zm'}, use_global_device_ids=true, to_apply=%region_2.3 | all-reduce | flops 2048 | bytes 16384 | tf_op jit(solution)/shard_map/psum | solution.py:224
  93.9 0.1 bitcast_add_fusion
  94.0 7.0 %collective-permute-start.2 = (bf16[144,256]{1,0:T(8,128)(2,1)S(1)}, bf16[144,256]{1,0:T(8,128)(2,1)S(1)}, u32[]{:S(2)}, u32[]{:S(2)}) collective-permute-start(bf16[144,256]{1,0:T(8,128)(2,1)S(1)} %get-tuple-element.27), channel_id=1, source_target_pairs={{0,8},{4,12},{8,0},{12,4},{1,9},{5,13},{9,1},{13,5},{2,10},{6,14},... | collective-permute-start | bytes 221192 | tf_op jit(solution)/shard_map/ppermute | solution.py:234
  101.0 4.9 %collective-permute-start.3 = (bf16[144,256]{1,0:T(8,128)(2,1)S(1)}, bf16[144,256]{1,0:T(8,128)(2,1)S(1)}, u32[]{:S(2)}, u32[]{:S(2)}) collective-permute-start(bf16[144,256]{1,0:T(8,128)(2,1)S(1)} %get-tuple-element.28), channel_id=1, source_target_pairs={{0,4},{4,8},{8,12},{12,0},{1,5},{5,9},{9,13},{13,1},{2,6},{6,10},{... | collective-permute-start | bytes 221192 | tf_op jit(solution)/shard_map/ppermute | solution.py:234
  106.0 4.3 %collective-permute-start.4 = (bf16[144,256]{1,0:T(8,128)(2,1)S(1)}, bf16[144,256]{1,0:T(8,128)(2,1)S(1)}, u32[]{:S(2)}, u32[]{:S(2)}) collective-permute-start(bf16[144,256]{1,0:T(8,128)(2,1)S(1)} %get-tuple-element.29), channel_id=1, source_target_pairs={{0,12},{4,0},{8,4},{12,8},{1,13},{5,1},{9,5},{13,9},{2,14},{6,2},{... | collective-permute-start | bytes 221192 | tf_op jit(solution)/shard_map/ppermute | solution.py:234
  110.3 4.7 %collective-permute-done.3 = bf16[144,256]{1,0:T(8,128)(2,1)S(1)} collective-permute-done((bf16[144,256]{1,0:T(8,128)(2,1)S(1)}, bf16[144,256]{1,0:T(8,128)(2,1)S(1)}, u32[]{:S(2)}, u32[]{:S(2)}) %collective-permute-start.3) | collective-permute-done | bytes 73760 | tf_op jit(solution)/shard_map/ppermute | solution.py:234
  114.9 4.7 %collective-permute-done.4 = bf16[144,256]{1,0:T(8,128)(2,1)S(1)} collective-permute-done((bf16[144,256]{1,0:T(8,128)(2,1)S(1)}, bf16[144,256]{1,0:T(8,128)(2,1)S(1)}, u32[]{:S(2)}, u32[]{:S(2)}) %collective-permute-start.4) | collective-permute-done | bytes 73760 | tf_op jit(solution)/shard_map/ppermute | solution.py:234
  119.7 0.7 fusion.9
  120.3 0.6 fusion.10
  (23 shorter events, 0.2 us)
Async XLA Ops:
  0.6 29.8 %copy-start = (s32[1,32]{1,0:T(1,128)S(1)}, s32[1,32]{1,0:T(1,128)}, u32[]{:S(2)}) copy-start(s32[1,32]{1,0:T(1,128)} %param.9) | copy-start | bytes 388
  0.6 25.6 %copy-start.4 = (bf16[1,128,256]{2,1,0:T(8,128)(2,1)S(1)}, bf16[1,128,256]{2,1,0:T(8,128)(2,1)}, u32[]{:S(2)}) copy-start(bf16[1,128,256]{2,1,0:T(8,128)(2,1)} %param.5) | copy-start | bytes 196612
  27.0 21.6 %all-to-all-start = ((bf16[4,128,256]{2,1,0:T(8,128)(2,1)}), bf16[4,128,256]{2,1,0:T(8,128)(2,1)S(1)}, u32[]{:S(2)}, u32[]{:S(2)}) async-start(bf16[4,128,256]{2,1,0:T(8,128)(2,1)} %broadcast_in_dim.6), calls=%async_computation | async-start | bytes 524288 | tf_op jit(solution)/shard_map/all_to_all | solution.py:208
  30.7 18.0 %copy-start.1 = (bf16[1,128,1024]{2,1,0:T(8,128)(2,1)S(1)}, bf16[1,128,1024]{2,1,0:T(8,128)(2,1)}, u32[]{:S(2)}) copy-start(bf16[1,128,1024]{2,1,0:T(8,128)(2,1)} %param.6) | copy-start | bytes 786436
  30.7 17.9 %copy-start.2 = (bf16[1,128,1024]{2,1,0:T(8,128)(2,1)S(1)}, bf16[1,128,1024]{2,1,0:T(8,128)(2,1)}, u32[]{:S(2)}) copy-start(bf16[1,128,1024]{2,1,0:T(8,128)(2,1)} %param.8) | copy-start | bytes 786436
  30.7 17.9 %copy-start.3 = (bf16[1,128,256]{2,1,0:T(8,128)(2,1)S(1)}, bf16[1,128,256]{2,1,0:T(8,128)(2,1)}, u32[]{:S(2)}) copy-start(bf16[1,128,256]{2,1,0:T(8,128)(2,1)} %param.7) | copy-start | bytes 196612
  56.4 15.7 %collective-permute-start = (bf16[1024,256]{1,0:T(8,128)(2,1)S(1)}, bf16[1024,256]{1,0:T(8,128)(2,1)S(1)}, u32[]{:S(2)}, u32[]{:S(2)}) collective-permute-start(bf16[1024,256]{1,0:T(8,128)(2,1)S(1)} %get-tuple-element.16), channel_id=1, source_target_pairs={{0,1},{1,0},{2,3},{3,2},{4,5},{5,4},{6,7},{7,6},{8,9},{9,8},{10,11... | collective-permute-start | bytes 1572872 | tf_op jit(solution)/shard_map/ppermute | solution.py:216
  59.2 21.9 %all-to-all-start.1 = ((f32[32,16,128]{2,1,0:T(8,128)}), f32[32,16,128]{2,1,0:T(8,128)S(1)}, u32[]{:S(2)}, u32[]{:S(2)}) async-start(f32[32,16,128]{2,1,0:T(8,128)} %get-tuple-element.17), calls=%async_computation.1 | async-start | bytes 524288 | tf_op jit(solution)/shard_map/all_to_all | solution.py:217
  72.3 21.6 %collective-permute-start.1 = (bf16[4,128,256]{2,1,0:T(8,128)(2,1)S(1)}, bf16[4,128,256]{2,1,0:T(8,128)(2,1)S(1)}, u32[]{:S(2)}, u32[]{:S(2)}) collective-permute-start(bf16[4,128,256]{2,1,0:T(8,128)(2,1)S(1)} %fusion), channel_id=1, source_target_pairs={{0,2},{2,0},{1,3},{3,1},{4,6},{6,4},{5,7},{7,5},{8,10},{10,8},{9,1... | collective-permute-start | bytes 786440 | tf_op jit(solution)/shard_map/ppermute | solution.py:221
  94.0 16.2 %collective-permute-start.2 = (bf16[144,256]{1,0:T(8,128)(2,1)S(1)}, bf16[144,256]{1,0:T(8,128)(2,1)S(1)}, u32[]{:S(2)}, u32[]{:S(2)}) collective-permute-start(bf16[144,256]{1,0:T(8,128)(2,1)S(1)} %get-tuple-element.27), channel_id=1, source_target_pairs={{0,8},{4,12},{8,0},{12,4},{1,9},{5,13},{9,1},{13,5},{2,10},{6,14},... | collective-permute-start | bytes 221192 | tf_op jit(solution)/shard_map/ppermute | solution.py:234
  101.0 13.9 %collective-permute-start.3 = (bf16[144,256]{1,0:T(8,128)(2,1)S(1)}, bf16[144,256]{1,0:T(8,128)(2,1)S(1)}, u32[]{:S(2)}, u32[]{:S(2)}) collective-permute-start(bf16[144,256]{1,0:T(8,128)(2,1)S(1)} %get-tuple-element.28), channel_id=1, source_target_pairs={{0,4},{4,8},{8,12},{12,0},{1,5},{5,9},{9,13},{13,1},{2,6},{6,10},{... | collective-permute-start | bytes 221192 | tf_op jit(solution)/shard_map/ppermute | solution.py:234
  106.0 13.7 %collective-permute-start.4 = (bf16[144,256]{1,0:T(8,128)(2,1)S(1)}, bf16[144,256]{1,0:T(8,128)(2,1)S(1)}, u32[]{:S(2)}, u32[]{:S(2)}) collective-permute-start(bf16[144,256]{1,0:T(8,128)(2,1)S(1)} %get-tuple-element.29), channel_id=1, source_target_pairs={{0,12},{4,0},{8,4},{12,8},{1,13},{5,1},{9,5},{13,9},{2,14},{6,2},{... | collective-permute-start | bytes 221192 | tf_op jit(solution)/shard_map/ppermute | solution.py:234

commit v5 on v4

--- a/solution.py
+++ b/solution.py
@@ -221,7 +221,7 @@
     got = lax.ppermute(away, "zm", SWAP)
     bias, away = lax.optimization_barrier((bias, away))
     bias = bias.sum(0)
-    bias = lax.psum(lax.psum(bias, "zl"), "zm")
+    bias = lax.psum(bias, QUAD)
     high = bias.astype(BF16)
     low = (bias - high.astype(F32)).astype(BF16)
     extra = jnp.concatenate([high, low], 1)

time: 121 us -> 118 us (0.975)
  blocking collectives: 56.3 us -> 53.2 us
    psum x2 -> x1, blocking collectives: 12.8 us -> 9.66 us  [body(): bias = lax.psum(bias, QUAD)]
where the time goes in v5:
time: 118 us
  blocking collectives  53.2 us (45%)
  starting transfers between devices  39.5 us (33%)
  waiting for transfers between devices  13.8 us (12%)
  Pallas kernels  7.76 us (7%)
  other arithmetic  1.72 us (1%)
    all_gather x1, blocking collectives, body(): column = lax.all_gather(mine, 'zh')  25.6 us
    all_gather x1, blocking collectives, body(): far = lax.all_gather(others.reshape(-1, 256), QUAD, axis=0, tiled=True)  17.9 us
    ppermute x3, starting transfers between devices, body(): lax.ppermute(sent, 'zh', [(p, (p + far) % n) for p in range(n)]).astype(F32)  16.2 us
    all_to_all x1, starting transfers between devices, body(): bias = lax.all_to_all(bias, DP, 0, 0, tiled=True)  12.9 us
    psum x1, blocking collectives, body(): bias = lax.psum(bias, QUAD)  9.66 us
    ppermute x3, waiting for transfers between devices, body(): lax.ppermute(sent, 'zh', [(p, (p + far) % n) for p in range(n)]).astype(F32)  9.27 us
    pallas_call x1, Pallas kernels, grads(): pl.pallas_call(grads_kernel, out_shape=(jax.ShapeDtypeStruct((rows, width...  7.76 us
    all_to_all x1, waiting for transfers between devices, body(): bias = lax.all_to_all(bias, DP, 0, 0, tiled=True)  4.49 us
  transfers between devices with their start and end apart: 7, of which 3 were waited for; matrix products, arithmetic and copies ran while one was open for 0% of the time, Pallas kernels for 0%

profile of v5, /device:TPU:1, one launch (start us, length us, event | category | flops | bytes accessed | tf_op | source)
XLA Modules:
  0.0 117.7 jit_solution(10299651747566810154)
XLA Ops:
  0.6 0.0 copy-start
  0.7 25.6 %all_gather.6 = bf16[4,128,256]{2,1,0:T(8,128)(2,1)S(1)} all-gather(bf16[1,128,256]{2,1,0:T(8,128)(2,1)} %param.5), channel_id=1, replica_groups=mesh['x'=4,'y'=4,'c'=2,'zh'=4,'zm'=2,'zl'=2] {'zh'}, dimensions={0}, use_global_device_ids=true | all-gather | bytes 327680 | tf_op jit(solution)/shard_map/all_gather | solution.py:206
  26.3 0.7 broadcast_in_dim.6
  27.0 3.4 %all-to-all-start = ((bf16[4,128,256]{2,1,0:T(8,128)(2,1)}), bf16[4,128,256]{2,1,0:T(8,128)(2,1)S(1)}, u32[]{:S(2)}, u32[]{:S(2)}) async-start(bf16[4,128,256]{2,1,0:T(8,128)(2,1)} %broadcast_in_dim.6), calls=%async_computation | async-start | bytes 524288 | tf_op jit(solution)/shard_map/all_to_all | solution.py:208
  30.4 0.1 fusion.11
  30.5 0.1 pad_add_fusion.info
  30.6 0.1 fusion.1
  30.7 0.0 copy-start.1
  30.7 17.9 %all_gather.7.far_ref = bf16[1536,256]{1,0:T(8,128)(2,1)S(1)} all-gather(bf16[384,256]{1,0:T(8,128)(2,1)S(1)} %bitcast.41), channel_id=1, replica_groups=mesh['x'=4,'y'=4,'c'=2,'zh'=4,'zm'=2,'zl'=2] {'zm','zl'}, dimensions={0}, use_global_device_ids=true | all-gather | bytes 983040 | tf_op jit(solution)/shard_map/all_gather | solution.py:210
  48.6 7.8 %shard_map.84 = (bf16[128,1024]{1,0:T(8,128)(2,1)}, bf16[128,256]{1,0:T(8,128)(2,1)}, bf16[1024,256]{1,0:T(8,128)(2,1)S(1)}, f32[1024,256]{1,0:T(8,128)S(1)}, f32[32,16,128]{2,1,0:T(8,128)}) custom-call(s32[4]{0:T(128)S(1)} %pad_add_fusion.info, bf16[128,1024]{1,0:T(8,128)(2,1)S(1)} %bitcast.36, bf16[128,1024]{1,0:T(8,128)(2,1)S(1)} %bitcast.37, ...), custom_call_target="tpu_custom_call" | custom-call | flops 2684354560 | bytes 3145728 | tf_op jit(solution)/shard_map/pallas_call | solution.py:166
  56.4 2.7 %collective-permute-start = (bf16[1024,256]{1,0:T(8,128)(2,1)S(1)}, bf16[1024,256]{1,0:T(8,128)(2,1)S(1)}, u32[]{:S(2)}, u32[]{:S(2)}) collective-permute-start(bf16[1024,256]{1,0:T(8,128)(2,1)S(1)} %get-tuple-element.16), channel_id=1, source_target_pairs={{0,1},{1,0},{2,3},{3,2},{4,5},{5,4},{6,7},{7,6},{8,9},{9,8},{10,11... | collective-permute-start | bytes 1572872 | tf_op jit(solution)/shard_map/ppermute | solution.py:216
  59.1 12.9 %all-to-all-start.1 = ((f32[32,16,128]{2,1,0:T(8,128)}), f32[32,16,128]{2,1,0:T(8,128)S(1)}, u32[]{:S(2)}, u32[]{:S(2)}) async-start(f32[32,16,128]{2,1,0:T(8,128)} %get-tuple-element.17), calls=%async_computation.1 | async-start | bytes 524288 | tf_op jit(solution)/shard_map/all_to_all | solution.py:217
  72.1 0.1 convert_add_fusion
  72.3 4.3 %collective-permute-start.1 = (bf16[4,128,256]{2,1,0:T(8,128)(2,1)S(1)}, bf16[4,128,256]{2,1,0:T(8,128)(2,1)S(1)}, u32[]{:S(2)}, u32[]{:S(2)}) collective-permute-start(bf16[4,128,256]{2,1,0:T(8,128)(2,1)S(1)} %fusion), channel_id=1, source_target_pairs={{0,2},{2,0},{1,3},{3,1},{4,6},{6,4},{5,7},{7,5},{8,10},{10,8},{9,1... | collective-permute-start | bytes 786440 | tf_op jit(solution)/shard_map/ppermute | solution.py:221
  76.6 4.5 %all-to-all-done.1 = f32[32,16,128]{2,1,0:T(8,128)S(1)} async-done(((f32[32,16,128]{2,1,0:T(8,128)}), f32[32,16,128]{2,1,0:T(8,128)S(1)}, u32[]{:S(2)}, u32[]{:S(2)}) %all-to-all-start.1) | async-done | bytes 262176 | tf_op jit(solution)/shard_map/all_to_all | solution.py:217
  81.1 9.7 %psum.7 = f32[16,128]{1,0:T(8,128)S(1)} all-reduce(f32[16,128]{1,0:T(8,128)S(1)} %reduce_sum.9), channel_id=1, replica_groups=mesh['x'=4,'y'=4,'c'=2,'zh'=4,'zm'=2,'zl'=2] {'zm','zl'}, use_global_device_ids=true, to_apply=%region_1.2 | all-reduce | flops 2048 | bytes 16384 | tf_op jit(solution)/shard_map/psum | solution.py:224
  90.8 0.1 bitcast_add_fusion
  90.9 7.0 %collective-permute-start.2 = (bf16[144,256]{1,0:T(8,128)(2,1)S(1)}, bf16[144,256]{1,0:T(8,128)(2,1)S(1)}, u32[]{:S(2)}, u32[]{:S(2)}) collective-permute-start(bf16[144,256]{1,0:T(8,128)(2,1)S(1)} %get-tuple-element.27), channel_id=1, source_target_pairs={{0,8},{4,12},{8,0},{12,4},{1,9},{5,13},{9,1},{13,5},{2,10},{6,14},... | collective-permute-start | bytes 221192 | tf_op jit(solution)/shard_map/ppermute | solution.py:234
  97.9 4.9 %collective-permute-start.3 = (bf16[144,256]{1,0:T(8,128)(2,1)S(1)}, bf16[144,256]{1,0:T(8,128)(2,1)S(1)}, u32[]{:S(2)}, u32[]{:S(2)}) collective-permute-start(bf16[144,256]{1,0:T(8,128)(2,1)S(1)} %get-tuple-element.28), channel_id=1, source_target_pairs={{0,4},{4,8},{8,12},{12,0},{1,5},{5,9},{9,13},{13,1},{2,6},{6,10},{... | collective-permute-start | bytes 221192 | tf_op jit(solution)/shard_map/ppermute | solution.py:234
  102.8 4.3 %collective-permute-start.4 = (bf16[144,256]{1,0:T(8,128)(2,1)S(1)}, bf16[144,256]{1,0:T(8,128)(2,1)S(1)}, u32[]{:S(2)}, u32[]{:S(2)}) collective-permute-start(bf16[144,256]{1,0:T(8,128)(2,1)S(1)} %get-tuple-element.29), channel_id=1, source_target_pairs={{0,12},{4,0},{8,4},{12,8},{1,13},{5,1},{9,5},{13,9},{2,14},{6,2},{... | collective-permute-start | bytes 221192 | tf_op jit(solution)/shard_map/ppermute | solution.py:234
  107.1 4.7 %collective-permute-done.3 = bf16[144,256]{1,0:T(8,128)(2,1)S(1)} collective-permute-done((bf16[144,256]{1,0:T(8,128)(2,1)S(1)}, bf16[144,256]{1,0:T(8,128)(2,1)S(1)}, u32[]{:S(2)}, u32[]{:S(2)}) %collective-permute-start.3) | collective-permute-done | bytes 73760 | tf_op jit(solution)/shard_map/ppermute | solution.py:234
  111.8 4.6 %collective-permute-done.4 = bf16[144,256]{1,0:T(8,128)(2,1)S(1)} collective-permute-done((bf16[144,256]{1,0:T(8,128)(2,1)S(1)}, bf16[144,256]{1,0:T(8,128)(2,1)S(1)}, u32[]{:S(2)}, u32[]{:S(2)}) %collective-permute-start.4) | collective-permute-done | bytes 73760 | tf_op jit(solution)/shard_map/ppermute | solution.py:234
  116.5 0.7 fusion.9
  117.1 0.6 fusion.10
  (22 shorter events, 0.2 us)
Async XLA Ops:
  0.6 29.8 %copy-start = (s32[1,32]{1,0:T(1,128)S(1)}, s32[1,32]{1,0:T(1,128)}, u32[]{:S(2)}) copy-start(s32[1,32]{1,0:T(1,128)} %param.9) | copy-start | bytes 388
  0.6 25.6 %copy-start.4 = (bf16[1,128,256]{2,1,0:T(8,128)(2,1)S(1)}, bf16[1,128,256]{2,1,0:T(8,128)(2,1)}, u32[]{:S(2)}) copy-start(bf16[1,128,256]{2,1,0:T(8,128)(2,1)} %param.5) | copy-start | bytes 196612
  27.0 21.6 %all-to-all-start = ((bf16[4,128,256]{2,1,0:T(8,128)(2,1)}), bf16[4,128,256]{2,1,0:T(8,128)(2,1)S(1)}, u32[]{:S(2)}, u32[]{:S(2)}) async-start(bf16[4,128,256]{2,1,0:T(8,128)(2,1)} %broadcast_in_dim.6), calls=%async_computation | async-start | bytes 524288 | tf_op jit(solution)/shard_map/all_to_all | solution.py:208
  30.7 18.0 %copy-start.1 = (bf16[1,128,1024]{2,1,0:T(8,128)(2,1)S(1)}, bf16[1,128,1024]{2,1,0:T(8,128)(2,1)}, u32[]{:S(2)}) copy-start(bf16[1,128,1024]{2,1,0:T(8,128)(2,1)} %param.6) | copy-start | bytes 786436
  30.7 17.9 %copy-start.2 = (bf16[1,128,1024]{2,1,0:T(8,128)(2,1)S(1)}, bf16[1,128,1024]{2,1,0:T(8,128)(2,1)}, u32[]{:S(2)}) copy-start(bf16[1,128,1024]{2,1,0:T(8,128)(2,1)} %param.8) | copy-start | bytes 786436
  30.7 17.9 %copy-start.3 = (bf16[1,128,256]{2,1,0:T(8,128)(2,1)S(1)}, bf16[1,128,256]{2,1,0:T(8,128)(2,1)}, u32[]{:S(2)}) copy-start(bf16[1,128,256]{2,1,0:T(8,128)(2,1)} %param.7) | copy-start | bytes 196612
  56.4 15.7 %collective-permute-start = (bf16[1024,256]{1,0:T(8,128)(2,1)S(1)}, bf16[1024,256]{1,0:T(8,128)(2,1)S(1)}, u32[]{:S(2)}, u32[]{:S(2)}) collective-permute-start(bf16[1024,256]{1,0:T(8,128)(2,1)S(1)} %get-tuple-element.16), channel_id=1, source_target_pairs={{0,1},{1,0},{2,3},{3,2},{4,5},{5,4},{6,7},{7,6},{8,9},{9,8},{10,11... | collective-permute-start | bytes 1572872 | tf_op jit(solution)/shard_map/ppermute | solution.py:216
  59.1 21.9 %all-to-all-start.1 = ((f32[32,16,128]{2,1,0:T(8,128)}), f32[32,16,128]{2,1,0:T(8,128)S(1)}, u32[]{:S(2)}, u32[]{:S(2)}) async-start(f32[32,16,128]{2,1,0:T(8,128)} %get-tuple-element.17), calls=%async_computation.1 | async-start | bytes 524288 | tf_op jit(solution)/shard_map/all_to_all | solution.py:217
  72.3 18.5 %collective-permute-start.1 = (bf16[4,128,256]{2,1,0:T(8,128)(2,1)S(1)}, bf16[4,128,256]{2,1,0:T(8,128)(2,1)S(1)}, u32[]{:S(2)}, u32[]{:S(2)}) collective-permute-start(bf16[4,128,256]{2,1,0:T(8,128)(2,1)S(1)} %fusion), channel_id=1, source_target_pairs={{0,2},{2,0},{1,3},{3,1},{4,6},{6,4},{5,7},{7,5},{8,10},{10,8},{9,1... | collective-permute-start | bytes 786440 | tf_op jit(solution)/shard_map/ppermute | solution.py:221
  90.9 16.2 %collective-permute-start.2 = (bf16[144,256]{1,0:T(8,128)(2,1)S(1)}, bf16[144,256]{1,0:T(8,128)(2,1)S(1)}, u32[]{:S(2)}, u32[]{:S(2)}) collective-permute-start(bf16[144,256]{1,0:T(8,128)(2,1)S(1)} %get-tuple-element.27), channel_id=1, source_target_pairs={{0,8},{4,12},{8,0},{12,4},{1,9},{5,13},{9,1},{13,5},{2,10},{6,14},... | collective-permute-start | bytes 221192 | tf_op jit(solution)/shard_map/ppermute | solution.py:234
  97.9 13.9 %collective-permute-start.3 = (bf16[144,256]{1,0:T(8,128)(2,1)S(1)}, bf16[144,256]{1,0:T(8,128)(2,1)S(1)}, u32[]{:S(2)}, u32[]{:S(2)}) collective-permute-start(bf16[144,256]{1,0:T(8,128)(2,1)S(1)} %get-tuple-element.28), channel_id=1, source_target_pairs={{0,4},{4,8},{8,12},{12,0},{1,5},{5,9},{9,13},{13,1},{2,6},{6,10},{... | collective-permute-start | bytes 221192 | tf_op jit(solution)/shard_map/ppermute | solution.py:234
  102.8 13.6 %collective-permute-start.4 = (bf16[144,256]{1,0:T(8,128)(2,1)S(1)}, bf16[144,256]{1,0:T(8,128)(2,1)S(1)}, u32[]{:S(2)}, u32[]{:S(2)}) collective-permute-start(bf16[144,256]{1,0:T(8,128)(2,1)S(1)} %get-tuple-element.29), channel_id=1, source_target_pairs={{0,12},{4,0},{8,4},{12,8},{1,13},{5,1},{9,5},{13,9},{2,14},{6,2},{... | collective-permute-start | bytes 221192 | tf_op jit(solution)/shard_map/ppermute | solution.py:234

commit v6 on v5

--- a/solution.py
+++ b/solution.py
@@ -12,7 +12,7 @@
 BLK = 64
 KBLK = 128
 ORDER = (2, 1, 3)
-BP = 512
+BP = 1024
 NEG = -1e30
 DP = ("x", "y", "c")
 QUAD = ("zm", "zl")
@@ -86,7 +86,7 @@
                 w_s[pl.ds(unit, 1), cols] = (e * du).sum(0, keepdims=True)
         return carry
 
-    lax.fori_loop(0, nblk, first, 0, unroll=4)
+    lax.fori_loop(0, nblk, first, 0, unroll=2)
 
     own = []
     row_in = lax.broadcasted_iota(jnp.int32, (BLK, wide), 1) % BLK
@@ -142,7 +142,7 @@
         return (sum_k + dk.sum(0, keepdims=True), sum_v + dv.sum(0, keepdims=True))
 
     start = (sum(o[0] for o in own), sum(o[1] for o in own))
-    sum_k, sum_v = lax.fori_loop(0, nblk, second, start, unroll=4)
+    sum_k, sum_v = lax.fori_loop(0, nblk, second, start, unroll=2)
     parts = []
     dq = acc[...].T * scale
     for h in range(heads):

time: 118 us -> 119 us (level)
  no operation moved by 1% of the time
where the time goes in v6:
time: 119 us; the launch traced here: 118 us
  blocking collectives  53.2 us (45%)
  starting transfers between devices  39.5 us (33%)
  waiting for transfers between devices  13.7 us (12%)
  Pallas kernels  8.15 us (7%)
  other arithmetic  1.72 us (1%)
    all_gather x1, blocking collectives, body(): column = lax.all_gather(mine, 'zh')  25.6 us
    all_gather x1, blocking collectives, body(): far = lax.all_gather(others.reshape(-1, 256), QUAD, axis=0, tiled=True)  17.9 us
    ppermute x3, starting transfers between devices, body(): lax.ppermute(sent, 'zh', [(p, (p + far) % n) for p in range(n)]).astype(F32)  16.2 us
    all_to_all x1, starting transfers between devices, body(): bias = lax.all_to_all(bias, DP, 0, 0, tiled=True)  12.9 us
    psum x1, blocking collectives, body(): bias = lax.psum(bias, QUAD)  9.65 us
    ppermute x3, waiting for transfers between devices, body(): lax.ppermute(sent, 'zh', [(p, (p + far) % n) for p in range(n)]).astype(F32)  9.22 us
    pallas_call x1, Pallas kernels, grads(): pl.pallas_call(grads_kernel, out_shape=(jax.ShapeDtypeStruct((rows, width...  8.15 us
    all_to_all x1, waiting for transfers between devices, body(): bias = lax.all_to_all(bias, DP, 0, 0, tiled=True)  4.5 us
  transfers between devices with their start and end apart: 7, of which 3 were waited for; matrix products, arithmetic and copies ran while one was open for 0% of the time, Pallas kernels for 0%

profile of v6, /device:TPU:1, one launch (start us, length us, event | category | flops | bytes accessed | tf_op | source)
XLA Modules:
  0.0 118.1 jit_solution(5322315339036154513)
XLA Ops:
  0.6 0.0 copy-start
  0.7 25.6 %all_gather.6 = bf16[4,128,256]{2,1,0:T(8,128)(2,1)S(1)} all-gather(bf16[1,128,256]{2,1,0:T(8,128)(2,1)} %param.5), channel_id=1, replica_groups=mesh['x'=4,'y'=4,'c'=2,'zh'=4,'zm'=2,'zl'=2] {'zh'}, dimensions={0}, use_global_device_ids=true | all-gather | bytes 327680 | tf_op jit(solution)/shard_map/all_gather | solution.py:206
  26.3 0.7 broadcast_in_dim.6
  27.0 3.4 %all-to-all-start = ((bf16[4,128,256]{2,1,0:T(8,128)(2,1)}), bf16[4,128,256]{2,1,0:T(8,128)(2,1)S(1)}, u32[]{:S(2)}, u32[]{:S(2)}) async-start(bf16[4,128,256]{2,1,0:T(8,128)(2,1)} %broadcast_in_dim.6), calls=%async_computation | async-start | bytes 524288 | tf_op jit(solution)/shard_map/all_to_all | solution.py:208
  30.4 0.1 fusion.11
  30.5 0.1 pad_add_fusion.info
  30.6 0.1 fusion.1
  30.7 0.0 copy-start.1
  30.7 17.9 %all_gather.7.far_ref = bf16[1536,256]{1,0:T(8,128)(2,1)S(1)} all-gather(bf16[384,256]{1,0:T(8,128)(2,1)S(1)} %bitcast.41), channel_id=1, replica_groups=mesh['x'=4,'y'=4,'c'=2,'zh'=4,'zm'=2,'zl'=2] {'zm','zl'}, dimensions={0}, use_global_device_ids=true | all-gather | bytes 983040 | tf_op jit(solution)/shard_map/all_gather | solution.py:210
  48.6 8.2 %shard_map.84 = (bf16[128,1024]{1,0:T(8,128)(2,1)}, bf16[128,256]{1,0:T(8,128)(2,1)}, bf16[1024,256]{1,0:T(8,128)(2,1)S(1)}, f32[1024,256]{1,0:T(8,128)S(1)}, f32[32,16,128]{2,1,0:T(8,128)}) custom-call(s32[4]{0:T(128)S(1)} %pad_add_fusion.info, bf16[128,1024]{1,0:T(8,128)(2,1)S(1)} %bitcast.36, bf16[128,1024]{1,0:T(8,128)(2,1)S(1)} %bitcast.37, ...), custom_call_target="tpu_custom_call" | custom-call | flops 2684354560 | bytes 3145728 | tf_op jit(solution)/shard_map/pallas_call | solution.py:166
  56.8 2.7 %collective-permute-start = (bf16[1024,256]{1,0:T(8,128)(2,1)S(1)}, bf16[1024,256]{1,0:T(8,128)(2,1)S(1)}, u32[]{:S(2)}, u32[]{:S(2)}) collective-permute-start(bf16[1024,256]{1,0:T(8,128)(2,1)S(1)} %get-tuple-element.16), channel_id=1, source_target_pairs={{0,1},{1,0},{2,3},{3,2},{4,5},{5,4},{6,7},{7,6},{8,9},{9,8},{10,11... | collective-permute-start | bytes 1572872 | tf_op jit(solution)/shard_map/ppermute | solution.py:216
  59.5 12.9 %all-to-all-start.1 = ((f32[32,16,128]{2,1,0:T(8,128)}), f32[32,16,128]{2,1,0:T(8,128)S(1)}, u32[]{:S(2)}, u32[]{:S(2)}) async-start(f32[32,16,128]{2,1,0:T(8,128)} %get-tuple-element.17), calls=%async_computation.1 | async-start | bytes 524288 | tf_op jit(solution)/shard_map/all_to_all | solution.py:217
  72.5 0.1 convert_add_fusion
  72.7 4.2 %collective-permute-start.1 = (bf16[4,128,256]{2,1,0:T(8,128)(2,1)S(1)}, bf16[4,128,256]{2,1,0:T(8,128)(2,1)S(1)}, u32[]{:S(2)}, u32[]{:S(2)}) collective-permute-start(bf16[4,128,256]{2,1,0:T(8,128)(2,1)S(1)} %fusion), channel_id=1, source_target_pairs={{0,2},{2,0},{1,3},{3,1},{4,6},{6,4},{5,7},{7,5},{8,10},{10,8},{9,1... | collective-permute-start | bytes 786440 | tf_op jit(solution)/shard_map/ppermute | solution.py:221
  76.9 4.5 %all-to-all-done.1 = f32[32,16,128]{2,1,0:T(8,128)S(1)} async-done(((f32[32,16,128]{2,1,0:T(8,128)}), f32[32,16,128]{2,1,0:T(8,128)S(1)}, u32[]{:S(2)}, u32[]{:S(2)}) %all-to-all-start.1) | async-done | bytes 262176 | tf_op jit(solution)/shard_map/all_to_all | solution.py:217
  81.5 9.6 %psum.7 = f32[16,128]{1,0:T(8,128)S(1)} all-reduce(f32[16,128]{1,0:T(8,128)S(1)} %reduce_sum.9), channel_id=1, replica_groups=mesh['x'=4,'y'=4,'c'=2,'zh'=4,'zm'=2,'zl'=2] {'zm','zl'}, use_global_device_ids=true, to_apply=%region_1.2 | all-reduce | flops 2048 | bytes 16384 | tf_op jit(solution)/shard_map/psum | solution.py:224
  91.2 0.1 bitcast_add_fusion
  91.3 7.0 %collective-permute-start.2 = (bf16[144,256]{1,0:T(8,128)(2,1)S(1)}, bf16[144,256]{1,0:T(8,128)(2,1)S(1)}, u32[]{:S(2)}, u32[]{:S(2)}) collective-permute-start(bf16[144,256]{1,0:T(8,128)(2,1)S(1)} %get-tuple-element.27), channel_id=1, source_target_pairs={{0,8},{4,12},{8,0},{12,4},{1,9},{5,13},{9,1},{13,5},{2,10},{6,14},... | collective-permute-start | bytes 221192 | tf_op jit(solution)/shard_map/ppermute | solution.py:234
  98.3 4.9 %collective-permute-start.3 = (bf16[144,256]{1,0:T(8,128)(2,1)S(1)}, bf16[144,256]{1,0:T(8,128)(2,1)S(1)}, u32[]{:S(2)}, u32[]{:S(2)}) collective-permute-start(bf16[144,256]{1,0:T(8,128)(2,1)S(1)} %get-tuple-element.28), channel_id=1, source_target_pairs={{0,4},{4,8},{8,12},{12,0},{1,5},{5,9},{9,13},{13,1},{2,6},{6,10},{... | collective-permute-start | bytes 221192 | tf_op jit(solution)/shard_map/ppermute | solution.py:234
  103.2 4.3 %collective-permute-start.4 = (bf16[144,256]{1,0:T(8,128)(2,1)S(1)}, bf16[144,256]{1,0:T(8,128)(2,1)S(1)}, u32[]{:S(2)}, u32[]{:S(2)}) collective-permute-start(bf16[144,256]{1,0:T(8,128)(2,1)S(1)} %get-tuple-element.29), channel_id=1, source_target_pairs={{0,12},{4,0},{8,4},{12,8},{1,13},{5,1},{9,5},{13,9},{2,14},{6,2},{... | collective-permute-start | bytes 221192 | tf_op jit(solution)/shard_map/ppermute | solution.py:234
  107.5 4.7 %collective-permute-done.3 = bf16[144,256]{1,0:T(8,128)(2,1)S(1)} collective-permute-done((bf16[144,256]{1,0:T(8,128)(2,1)S(1)}, bf16[144,256]{1,0:T(8,128)(2,1)S(1)}, u32[]{:S(2)}, u32[]{:S(2)}) %collective-permute-start.3) | collective-permute-done | bytes 73760 | tf_op jit(solution)/shard_map/ppermute | solution.py:234
  112.2 4.5 %collective-permute-done.4 = bf16[144,256]{1,0:T(8,128)(2,1)S(1)} collective-permute-done((bf16[144,256]{1,0:T(8,128)(2,1)S(1)}, bf16[144,256]{1,0:T(8,128)(2,1)S(1)}, u32[]{:S(2)}, u32[]{:S(2)}) %collective-permute-start.4) | collective-permute-done | bytes 73760 | tf_op jit(solution)/shard_map/ppermute | solution.py:234
  116.8 0.7 fusion.9
  117.5 0.6 fusion.10
  (22 shorter events, 0.2 us)
Async XLA Ops:
  0.6 29.8 %copy-start = (s32[1,32]{1,0:T(1,128)S(1)}, s32[1,32]{1,0:T(1,128)}, u32[]{:S(2)}) copy-start(s32[1,32]{1,0:T(1,128)} %param.9) | copy-start | bytes 388
  0.6 25.6 %copy-start.4 = (bf16[1,128,256]{2,1,0:T(8,128)(2,1)S(1)}, bf16[1,128,256]{2,1,0:T(8,128)(2,1)}, u32[]{:S(2)}) copy-start(bf16[1,128,256]{2,1,0:T(8,128)(2,1)} %param.5) | copy-start | bytes 196612
  27.0 21.6 %all-to-all-start = ((bf16[4,128,256]{2,1,0:T(8,128)(2,1)}), bf16[4,128,256]{2,1,0:T(8,128)(2,1)S(1)}, u32[]{:S(2)}, u32[]{:S(2)}) async-start(bf16[4,128,256]{2,1,0:T(8,128)(2,1)} %broadcast_in_dim.6), calls=%async_computation | async-start | bytes 524288 | tf_op jit(solution)/shard_map/all_to_all | solution.py:208
  30.7 18.0 %copy-start.1 = (bf16[1,128,1024]{2,1,0:T(8,128)(2,1)S(1)}, bf16[1,128,1024]{2,1,0:T(8,128)(2,1)}, u32[]{:S(2)}) copy-start(bf16[1,128,1024]{2,1,0:T(8,128)(2,1)} %param.6) | copy-start | bytes 786436
  30.7 17.9 %copy-start.2 = (bf16[1,128,1024]{2,1,0:T(8,128)(2,1)S(1)}, bf16[1,128,1024]{2,1,0:T(8,128)(2,1)}, u32[]{:S(2)}) copy-start(bf16[1,128,1024]{2,1,0:T(8,128)(2,1)} %param.8) | copy-start | bytes 786436
  30.7 17.9 %copy-start.3 = (bf16[1,128,256]{2,1,0:T(8,128)(2,1)S(1)}, bf16[1,128,256]{2,1,0:T(8,128)(2,1)}, u32[]{:S(2)}) copy-start(bf16[1,128,256]{2,1,0:T(8,128)(2,1)} %param.7) | copy-start | bytes 196612
  56.8 15.7 %collective-permute-start = (bf16[1024,256]{1,0:T(8,128)(2,1)S(1)}, bf16[1024,256]{1,0:T(8,128)(2,1)S(1)}, u32[]{:S(2)}, u32[]{:S(2)}) collective-permute-start(bf16[1024,256]{1,0:T(8,128)(2,1)S(1)} %get-tuple-element.16), channel_id=1, source_target_pairs={{0,1},{1,0},{2,3},{3,2},{4,5},{5,4},{6,7},{7,6},{8,9},{9,8},{10,11... | collective-permute-start | bytes 1572872 | tf_op jit(solution)/shard_map/ppermute | solution.py:216
  59.5 21.9 %all-to-all-start.1 = ((f32[32,16,128]{2,1,0:T(8,128)}), f32[32,16,128]{2,1,0:T(8,128)S(1)}, u32[]{:S(2)}, u32[]{:S(2)}) async-start(f32[32,16,128]{2,1,0:T(8,128)} %get-tuple-element.17), calls=%async_computation.1 | async-start | bytes 524288 | tf_op jit(solution)/shard_map/all_to_all | solution.py:217
  72.7 18.5 %collective-permute-start.1 = (bf16[4,128,256]{2,1,0:T(8,128)(2,1)S(1)}, bf16[4,128,256]{2,1,0:T(8,128)(2,1)S(1)}, u32[]{:S(2)}, u32[]{:S(2)}) collective-permute-start(bf16[4,128,256]{2,1,0:T(8,128)(2,1)S(1)} %fusion), channel_id=1, source_target_pairs={{0,2},{2,0},{1,3},{3,1},{4,6},{6,4},{5,7},{7,5},{8,10},{10,8},{9,1... | collective-permute-start | bytes 786440 | tf_op jit(solution)/shard_map/ppermute | solution.py:221
  91.3 16.2 %collective-permute-start.2 = (bf16[144,256]{1,0:T(8,128)(2,1)S(1)}, bf16[144,256]{1,0:T(8,128)(2,1)S(1)}, u32[]{:S(2)}, u32[]{:S(2)}) collective-permute-start(bf16[144,256]{1,0:T(8,128)(2,1)S(1)} %get-tuple-element.27), channel_id=1, source_target_pairs={{0,8},{4,12},{8,0},{12,4},{1,9},{5,13},{9,1},{13,5},{2,10},{6,14},... | collective-permute-start | bytes 221192 | tf_op jit(solution)/shard_map/ppermute | solution.py:234
  98.3 13.9 %collective-permute-start.3 = (bf16[144,256]{1,0:T(8,128)(2,1)S(1)}, bf16[144,256]{1,0:T(8,128)(2,1)S(1)}, u32[]{:S(2)}, u32[]{:S(2)}) collective-permute-start(bf16[144,256]{1,0:T(8,128)(2,1)S(1)} %get-tuple-element.28), channel_id=1, source_target_pairs={{0,4},{4,8},{8,12},{12,0},{1,5},{5,9},{9,13},{13,1},{2,6},{6,10},{... | collective-permute-start | bytes 221192 | tf_op jit(solution)/shard_map/ppermute | solution.py:234
  103.2 13.5 %collective-permute-start.4 = (bf16[144,256]{1,0:T(8,128)(2,1)S(1)}, bf16[144,256]{1,0:T(8,128)(2,1)S(1)}, u32[]{:S(2)}, u32[]{:S(2)}) collective-permute-start(bf16[144,256]{1,0:T(8,128)(2,1)S(1)} %get-tuple-element.29), channel_id=1, source_target_pairs={{0,12},{4,0},{8,4},{12,8},{1,13},{5,1},{9,5},{13,9},{2,14},{6,2},{... | collective-permute-start | bytes 221192 | tf_op jit(solution)/shard_map/ppermute | solution.py:234
